TPU v7x, 32 devices: a whole 2x2x4 slice. The times are simulated.
32 devices in a mesh: dp: 4 (over y, x), seq: 8 (over z, core).
Axes of the slice: x: 2, y: 2, z: 4, core: 2. Of those that a mesh axis runs over, the one named last changes fastest.
Arguments:
- sequence: bfloat16 [16384, 1536], P(('dp', 'seq')), parts along dimension 0, may hold values from -6 to 6
- conv_weight: bfloat16 [5, 1536, 1536], replicated, may hold values from -0.0625 to 0.0625
- qkv_weight: bfloat16 [1536, 3072], P('seq'), may hold values from -2 to 2
- out_weight: bfloat16 [1024, 1536], P('seq'), may hold values from -4 to 4
Outputs:
- pooled: bfloat16 [8192, 1536], P(('dp', 'seq')), parts along dimension 0
- update: bfloat16 [8192, 1536], P(('dp', 'seq')), parts along dimension 0
There are 4 independent parts, one for each index of `dp`. A program takes and returns all parts, laid end to end along the dimension named above; an argument that names none is the same for every part. Nothing has to cross between parts.
All inputs are finite; a program needn't handle non-finite values.
Results may differ from a plain program's by a relative error of at most 0.0065.
Values may be sent and summed in bfloat16 or wider, within the bound.
A program may use at most 128 MiB of HBM per device.

v0:
```python
import jax
import jax.numpy as jnp
from jax import lax
from jax.sharding import PartitionSpec as P

HEADS = 8
HEAD_DIM = 128
WIDTH = 5


def with_halo(block, sides, width):
    for axis, dim in sides:
        count = lax.axis_size(axis)
        forward = [(i, i + 1) for i in range(count - 1)]
        backward = [(target, source) for source, target in forward]
        low = lax.ppermute(
            lax.slice_in_dim(block, block.shape[dim] - width, None, axis=dim), axis, forward
        )
        high = lax.ppermute(lax.slice_in_dim(block, 0, width, axis=dim), axis, backward)
        block = jnp.concatenate([low, block, high], axis=dim)
    return block


def normalize(values):
    return values * lax.rsqrt(jnp.mean(values * values, axis=-1, keepdims=True) + 1e-06)


def single_head(triple):
    query_rows, key_rows, value_rows = triple
    scores = jnp.dot(query_rows, key_rows.T, preferred_element_type=jnp.float32) * HEAD_DIM ** (
        -0.5
    )
    peak = jnp.max(scores, axis=-1, keepdims=True)
    expo = jnp.exp(scores - peak)
    total = jnp.sum(expo, axis=-1, keepdims=True)
    return (
        jnp.dot(expo.astype(jnp.bfloat16), value_rows, preferred_element_type=jnp.float32) / total
    ).astype(jnp.bfloat16)


def on_device(sequence, conv_weight, qkv_weight, out_weight):
    length = sequence.shape[0]
    inner = HEADS * HEAD_DIM
    extended = with_halo(sequence, (("seq", 0),), 2)
    activated = jax.nn.gelu(normalize(extended.astype(jnp.float32))).astype(jnp.bfloat16)
    mixed = sequence.astype(jnp.float32)
    for offset in range(WIDTH):
        mixed = mixed + jnp.dot(
            activated[offset : offset + length],
            conv_weight[offset],
            preferred_element_type=jnp.float32,
        )
    pooled = jnp.max(mixed.reshape(length // 2, 2, -1), axis=1).astype(jnp.bfloat16)
    count = pooled.shape[0]
    normed = normalize(pooled.astype(jnp.float32)).astype(jnp.bfloat16)
    columns = normed
    projected = jnp.dot(
        columns,
        lax.all_gather(qkv_weight, "seq", axis=0, tiled=True),
        preferred_element_type=jnp.float32,
    ).astype(jnp.bfloat16)
    seq_count = lax.axis_size("seq")
    groups = seq_count // HEADS
    share = count // groups
    query_send = (
        projected[:, :inner]
        .reshape(groups, share, HEADS, HEAD_DIM)
        .transpose(2, 0, 1, 3)
        .reshape(seq_count, share, HEAD_DIM)
    )
    pair_send = (
        projected[:, inner:]
        .reshape(count, 2, HEADS, HEAD_DIM)
        .transpose(2, 0, 1, 3)
        .reshape(HEADS, count, 2 * HEAD_DIM)
    )
    pair_send = jnp.repeat(pair_send, groups, axis=0)
    query_recv, pair_recv = (
        lax.all_to_all(query_send, "seq", split_axis=0, concat_axis=0, tiled=True),
        lax.all_to_all(pair_send, "seq", split_axis=0, concat_axis=0, tiled=True),
    )
    key_rows = pair_recv[:, :, :HEAD_DIM].reshape(seq_count * count, HEAD_DIM)
    value_rows = pair_recv[:, :, HEAD_DIM:].reshape(seq_count * count, HEAD_DIM)

    def per_source(query_rows):
        return single_head((query_rows, key_rows, value_rows))

    head_rows = lax.map(per_source, query_recv)
    returned = lax.all_to_all(head_rows, "seq", split_axis=0, concat_axis=0, tiled=True)
    attended = (
        returned.reshape(HEADS, groups, share, HEAD_DIM).transpose(1, 2, 0, 3).reshape(count, inner)
    )
    columns = attended
    update = jnp.dot(
        columns,
        lax.all_gather(out_weight, "seq", axis=0, tiled=True),
        preferred_element_type=jnp.float32,
    )
    return (pooled, update.astype(jnp.bfloat16))


def solution(mesh):
    return jax.shard_map(
        on_device,
        mesh=mesh,
        in_specs=(P(("dp", "seq"), None), P(), P("seq", None), P("seq", None)),
        out_specs=(P(("dp", "seq"), None), P(("dp", "seq"), None)),
        check_vma=False,
    )
```

profile of v0, /device:TPU:0, one launch (start us, length us, event | category | flops | bytes accessed | tf_op | source)
XLA Modules:
  0.0 208.8 jit_solution(8728402944748073098)
XLA Ops:
  7.2 0.7 all-gather.3.cloned.1.call-update
  7.9 0.8 fusion.58
  8.7 2.4 %collective-permute-start = (bf16[2,1536]{1,0:T(2,128)(2,1)S(1)}, bf16[2,1536]{1,0:T(2,128)(2,1)S(1)}, u32[]{:S(2)}, u32[]{:S(2)}) collective-permute-start(bf16[2,1536]{1,0:T(2,128)(2,1)S(1)} %get-tuple-element.42), channel_id=1, source_target_pairs={{0,1},{1,2},{2,3},{3,4},{4,5},{5,6},{6,7},{8,9},{9,10},{10,11},{11... | collective-permute-start | bytes 18440 | tf_op jit(solution)/shard_map/ppermute | solution.py:16
  11.0 1.3 collective-permute-start.1
  12.4 3.9 %collective-permute-done.1 = bf16[2,1536]{1,0:T(2,128)(2,1)S(1)} collective-permute-done((bf16[2,1536]{1,0:T(2,128)(2,1)S(1)}, bf16[2,1536]{1,0:T(2,128)(2,1)S(1)}, u32[]{:S(2)}, u32[]{:S(2)}) %collective-permute-start.1) | collective-permute-done | bytes 6176 | tf_op jit(solution)/shard_map/ppermute | solution.py:19
  16.3 2.0 fusion.46
  18.3 2.6 %fusion.41 = bf16[516,1536]{1,0:T(8,128)(2,1)S(1)} fusion(f32[516]{0:T(1024)S(1)} %add_rsqrt_fusion, bf16[2,1536]{1,0:T(2,128)(2,1)S(1)} %collective-permute-done.1, bf16[512,1536]{1,0:T(8,128)(2,1)S(1)} %copy-done, bf16[2,1536]{1,0:T(2,128)(2,1)S(1)} %collective-permute-done), kind=kLoop, calls=%fused_computation.38 | loop fusion | flops 12681216 | bytes 3172368 | tf_op jit(solution)/shard_map/convert_element_type | solution.py:45
  20.9 4.9 %fusion.13 = f32[512,1536]{1,0:T(8,128)S(1)} fusion(bf16[5,1536,1536]{2,1,0:T(8,128)(2,1)} %param.7, bf16[516,1536]{1,0:T(8,128)(2,1)S(1)} %fusion.41), kind=kOutput, calls=%fused_computation.17 | convolution fusion | flops 2415919104 | bytes 9437184 | tf_op jit(solution)/shard_map/dot_general | solution.py:48
  25.9 4.5 %fusion.15 = f32[512,1536]{1,0:T(8,128)S(1)} fusion(bf16[5,1536,1536]{2,1,0:T(8,128)(2,1)} %param.7, bf16[516,1536]{1,0:T(8,128)(2,1)S(1)} %fusion.41), kind=kOutput, calls=%fused_computation.19 | convolution fusion | flops 2415919104 | bytes 9437184 | tf_op jit(solution)/shard_map/dot_general | solution.py:48
  30.4 4.5 %fusion.11 = f32[512,1536]{1,0:T(8,128)S(1)} fusion(bf16[5,1536,1536]{2,1,0:T(8,128)(2,1)} %param.7, bf16[516,1536]{1,0:T(8,128)(2,1)S(1)} %fusion.41), kind=kOutput, calls=%fused_computation.15 | convolution fusion | flops 2415919104 | bytes 9437184 | tf_op jit(solution)/shard_map/dot_general | solution.py:48
  34.9 4.5 %fusion.9 = f32[512,1536]{1,0:T(8,128)S(1)} fusion(bf16[5,1536,1536]{2,1,0:T(8,128)(2,1)} %param.7, bf16[516,1536]{1,0:T(8,128)(2,1)S(1)} %fusion.41), kind=kOutput, calls=%fused_computation.13 | convolution fusion | flops 2415919104 | bytes 9437184 | tf_op jit(solution)/shard_map/dot_general | solution.py:48
  39.4 5.4 %fusion.38 = bf16[512,1536]{1,0:T(8,128)(2,1)S(1)} fusion(f32[512,1536]{1,0:T(8,128)S(1)} %fusion.9, f32[512,1536]{1,0:T(8,128)S(1)} %fusion.11, f32[512,1536]{1,0:T(8,128)S(1)} %fusion.13, f32[512,1536]{1,0:T(8,128)S(1)} %fusion.15, bf16[5,1536,1536]{2,1,0:T(8,128)(2,1)} %param.7, bf16[512,1536]{1,0:T(8,128)(2,1)S(1)} %copy-done, ...), kind=kOutput, calls=%fused_computation.37 | convolution fusion | flops 2421424128 | bytes 22020096 | tf_op jit(solution)/shard_map/dot_general | solution.py:48
  44.8 0.8 reshape.46
  45.6 4.3 %reduce_max.18 = bf16[256,1536]{1,0:T(8,128)(2,1)S(1)} reduce(bf16[256,2,1536]{2,1,0:T(2,128)(2,1)S(1)} %reshape.46, bf16[]{:T(256)} %constant.76), dimensions={1}, to_apply=%region_1.0 | reduce | flops 393216 | bytes 2359298 | tf_op jit(solution)/shard_map/reduce_max | solution.py:53
  50.2 53.0 %all-gather.3.cloned.1.call-done = bf16[1536,3072]{1,0:T(8,128)(2,1)} async-done(((bf16[192,3072]{1,0:T(8,128)(2,1)}), bf16[1536,3072]{1,0:T(8,128)(2,1)}) %all-gather.3.cloned.1.call-update) | async-done | bytes 9437200 | tf_op jit(solution)/shard_map/all_gather | solution.py:59
  103.1 6.4 %convolution_convert_fusion = bf16[256,3072]{1,0:T(8,128)(2,1)S(1)} fusion(bf16[1536,3072]{1,0:T(8,128)(2,1)} %all-gather.3.cloned.1.call-done, bf16[256,1536]{1,0:T(8,128)(2,1)S(1)} %reduce_max.18, f32[256]{0:T(256)S(1)} %add_rsqrt_fusion.1), kind=kOutput, calls=%fused_computation.32 | convolution fusion | flops 2417885184 | bytes 11797504 | tf_op jit(solution)/shard_map/dot_general | solution.py:57
  109.8 0.8 copy-done.2
  110.7 1.6 copy.11
  112.3 3.6 %all-to-all-start.1 = ((bf16[8,256,256]{1,2,0:T(8,128)(2,1)}), bf16[8,256,256]{1,2,0:T(8,128)(2,1)S(1)}, u32[]{:S(2)}, u32[]{:S(2)}) async-start(bf16[8,256,256]{1,2,0:T(8,128)(2,1)} %bitcast.10), calls=%async_computation.1 | async-start | bytes 2097152 | tf_op jit(solution)/shard_map/all_to_all | solution.py:80
  115.8 1.1 slice_bitcast_fusion.1
  117.0 0.9 copy.20
  117.9 24.5 %all-to-all-done.1 = bf16[8,256,256]{1,2,0:T(8,128)(2,1)S(1)} async-done(((bf16[8,256,256]{1,2,0:T(8,128)(2,1)}), bf16[8,256,256]{1,2,0:T(8,128)(2,1)S(1)}, u32[]{:S(2)}, u32[]{:S(2)}) %all-to-all-start.1) | async-done | bytes 1048608 | tf_op jit(solution)/shard_map/all_to_all | solution.py:80
  142.4 3.5 %all-to-all-start = ((bf16[8,256,128]{2,1,0:T(8,128)(2,1)}), bf16[8,256,128]{2,1,0:T(8,128)(2,1)S(1)}, u32[]{:S(2)}, u32[]{:S(2)}) async-start(bf16[8,256,128]{2,1,0:T(8,128)(2,1)} %bitcast.59), calls=%async_computation | async-start | bytes 1048576 | tf_op jit(solution)/shard_map/all_to_all | solution.py:79
  145.9 0.7 all-gather.5.cloned.1.call-update
  147.3 14.0 %all-to-all-done = bf16[8,256,128]{2,1,0:T(8,128)(2,1)S(1)} async-done(((bf16[8,256,128]{2,1,0:T(8,128)(2,1)}), bf16[8,256,128]{2,1,0:T(8,128)(2,1)S(1)}, u32[]{:S(2)}, u32[]{:S(2)}) %all-to-all-start) | async-done | bytes 524320 | tf_op jit(solution)/shard_map/all_to_all | solution.py:79
  161.2 18.0 %while.10 = (s32[]{:T(128)}, bf16[8,256,128]{1,2,0:T(8,128)(2,1)}, bf16[8,256,128]{2,1,0:T(8,128)(2,1)S(1)}, bf16[2048,128]{1,0:T(8,128)(2,1)S(1)}, bf16[2048,128]{1,0:T(8,128)(2,1)S(1)}, /*index=5*/s32[]{:T(128)}) while((s32[]{:T(128)}, bf16[8,256,128]{1,2,0:T(8,128)(2,1)}, bf16[8,256,128]{2,1,0:T(8,128)(2,1)S(1)}, ...), condition=%wide.region_6.7_spmd, body=%wide.region_3.6_spmd.sunk | while | flops 271646208 | bytes 7738953 | solution.py:88
  162.2 0.5 fusion.76
  162.8 0.6 constant_dynamic-update-slice_fusion.2
  163.5 0.5 fusion.74
  164.4 0.5 fusion.76
  165.1 0.6 constant_dynamic-update-slice_fusion.2
  165.7 0.5 fusion.74
  166.7 0.5 fusion.76
  167.3 0.6 constant_dynamic-update-slice_fusion.2
  168.9 0.5 fusion.76
  169.6 0.6 constant_dynamic-update-slice_fusion.2
  171.2 0.5 fusion.76
  171.8 0.6 constant_dynamic-update-slice_fusion.2
  173.4 0.5 fusion.76
  174.1 0.6 constant_dynamic-update-slice_fusion.2
  175.7 0.5 fusion.76
  176.3 0.6 constant_dynamic-update-slice_fusion.2
  177.9 0.5 fusion.76
  178.6 0.6 constant_dynamic-update-slice_fusion.2
  179.2 3.6 %all-to-all-start.2 = ((bf16[8,256,128]{1,2,0:T(8,128)(2,1)}), bf16[8,256,128]{1,2,0:T(8,128)(2,1)S(1)}, u32[]{:S(2)}, u32[]{:S(2)}) async-start(bf16[8,256,128]{1,2,0:T(8,128)(2,1)} %get-tuple-element.29), calls=%async_computation.2 | async-start | bytes 1048576 | tf_op jit(solution)/shard_map/all_to_all | solution.py:89
  182.8 5.3 %all-gather.5.cloned.1.call-done = bf16[1024,1536]{1,0:T(8,128)(2,1)} async-done(((bf16[128,1536]{1,0:T(8,128)(2,1)}), bf16[1024,1536]{1,0:T(8,128)(2,1)}) %all-gather.5.cloned.1.call-update) | async-done | bytes 3145744 | tf_op jit(solution)/shard_map/all_gather | solution.py:96
  188.1 10.1 %all-to-all-done.2 = bf16[8,256,128]{1,2,0:T(8,128)(2,1)S(1)} async-done(((bf16[8,256,128]{1,2,0:T(8,128)(2,1)}), bf16[8,256,128]{1,2,0:T(8,128)(2,1)S(1)}, u32[]{:S(2)}, u32[]{:S(2)}) %all-to-all-start.2) | async-done | bytes 524320 | tf_op jit(solution)/shard_map/all_to_all | solution.py:89
  198.2 3.8 %convolution_convert_fusion.1 = bf16[256,1536]{1,0:T(8,128)(2,1)} fusion(bf16[256,1024]{0,1:T(8,128)(2,1)S(1)} %bitcast.72, bf16[1024,1536]{1,0:T(8,128)(2,1)} %all-gather.5.cloned.1.call-done), kind=kOutput, calls=%fused_computation.45 | convolution fusion | flops 805699584 | bytes 4456448 | tf_op jit(solution)/shard_map/dot_general | solution.py:94
  (40 shorter events, 8.8 us)
Async XLA Ops:
  7.2 11.2 %copy-start = (bf16[512,1536]{1,0:T(8,128)(2,1)S(1)}, bf16[512,1536]{1,0:T(8,128)(2,1)}, u32[]{:S(2)}) copy-start(bf16[512,1536]{1,0:T(8,128)(2,1)} %param.6) | copy-start | bytes 4718596
  7.2 95.9 %all-gather.3.cloned.1.call-start = ((), (), s32[]{:S(2)}) async-start(), calls=%async_computation.3 | async-start | bytes 10616832 | tf_op jit(solution)/shard_map/all_gather | solution.py:59
  8.7 3.7 %collective-permute-start = (bf16[2,1536]{1,0:T(2,128)(2,1)S(1)}, bf16[2,1536]{1,0:T(2,128)(2,1)S(1)}, u32[]{:S(2)}, u32[]{:S(2)}) collective-permute-start(bf16[2,1536]{1,0:T(2,128)(2,1)S(1)} %get-tuple-element.42), channel_id=1, source_target_pairs={{0,1},{1,2},{2,3},{3,4},{4,5},{5,6},{6,7},{8,9},{9,10},{10,11},{11... | collective-permute-start | bytes 18440 | tf_op jit(solution)/shard_map/ppermute | solution.py:16
  11.0 5.3 %collective-permute-start.1 = (bf16[2,1536]{1,0:T(2,128)(2,1)S(1)}, bf16[2,1536]{1,0:T(2,128)(2,1)S(1)}, u32[]{:S(2)}, u32[]{:S(2)}) collective-permute-start(bf16[2,1536]{1,0:T(2,128)(2,1)S(1)} %get-tuple-element.43), channel_id=1, source_target_pairs={{1,0},{2,1},{3,2},{4,3},{5,4},{6,5},{7,6},{9,8},{10,9},{11,10},{12... | collective-permute-start | bytes 18440 | tf_op jit(solution)/shard_map/ppermute | solution.py:19
  49.9 59.6 %copy-start.1 = (bf16[256,1536]{1,0:T(8,128)(2,1)}, bf16[256,1536]{1,0:T(8,128)(2,1)S(1)}, u32[]{:S(2)}) copy-start(bf16[256,1536]{1,0:T(8,128)(2,1)S(1)} %reduce_max.18) | copy-start | bytes 2359300
  109.5 1.2 copy-start.2
  112.3 30.1 %all-to-all-start.1 = ((bf16[8,256,256]{1,2,0:T(8,128)(2,1)}), bf16[8,256,256]{1,2,0:T(8,128)(2,1)S(1)}, u32[]{:S(2)}, u32[]{:S(2)}) async-start(bf16[8,256,256]{1,2,0:T(8,128)(2,1)} %bitcast.10), calls=%async_computation.1 | async-start | bytes 2097152 | tf_op jit(solution)/shard_map/all_to_all | solution.py:80
  142.4 18.9 %all-to-all-start = ((bf16[8,256,128]{2,1,0:T(8,128)(2,1)}), bf16[8,256,128]{2,1,0:T(8,128)(2,1)S(1)}, u32[]{:S(2)}, u32[]{:S(2)}) async-start(bf16[8,256,128]{2,1,0:T(8,128)(2,1)} %bitcast.59), calls=%async_computation | async-start | bytes 1048576 | tf_op jit(solution)/shard_map/all_to_all | solution.py:79
  145.9 42.3 %all-gather.5.cloned.1.call-start = ((), (), s32[]{:S(2)}) async-start(), calls=%async_computation.4 | async-start | bytes 3538944 | tf_op jit(solution)/shard_map/all_gather | solution.py:96
  179.2 19.0 %all-to-all-start.2 = ((bf16[8,256,128]{1,2,0:T(8,128)(2,1)}), bf16[8,256,128]{1,2,0:T(8,128)(2,1)S(1)}, u32[]{:S(2)}, u32[]{:S(2)}) async-start(bf16[8,256,128]{1,2,0:T(8,128)(2,1)} %get-tuple-element.29), calls=%async_computation.2 | async-start | bytes 1048576 | tf_op jit(solution)/shard_map/all_to_all | solution.py:89
Sparse Core Ops, SparseCore 0:
  9.7 93.4 all-gather.2
  148.3 39.7 all-gather.4
where the time goes:
time: 209 us
  waiting for transfers between devices  112 us (54%)
  matrix products  42.3 us (20%)
  starting transfers between devices  14.4 us (7%)
  between operations  14.2 us (7%)
  local copies, waits for them, and re-layouts  13 us (6%)
  other arithmetic  12.7 us (6%)
    all_gather x1, waiting for transfers between devices, on_device(): lax.all_gather(qkv_weight, 'seq', axis=0, tiled=True)  53 us
    all_to_all x1, waiting for transfers between devices, on_device(): lax.all_to_all(pair_send, 'seq', split_axis=0, concat_axis=0, tiled=True)  24.5 us
    dot_general x5, matrix products, on_device(): jnp.dot(activated[offset:offset + length], conv_weight[offset], preferred...  23.8 us
    all_to_all x1, waiting for transfers between devices, on_device(): lax.all_to_all(query_send, 'seq', split_axis=0, concat_axis=0, tiled=True)  14 us
    all_to_all x1, waiting for transfers between devices, on_device(): lax.all_to_all(head_rows, 'seq', split_axis=0, concat_axis=0, tiled=True)  10.1 us
    dot_general x1, matrix products, on_device(): jnp.dot(columns, lax.all_gather(qkv_weight, 'seq', axis=0, tiled=True), p...  6.38 us
    dynamic_update_slice x16, local copies, waits for them, and re-layouts, on_device(): head_rows = lax.map(per_source, query_recv)  5.97 us
    all_gather x1, waiting for transfers between devices, on_device(): lax.all_gather(out_weight, 'seq', axis=0, tiled=True)  5.28 us
  transfers between devices with their start and end apart: 7, of which 6 were waited for; matrix products, arithmetic and copies ran while one was open for 26% of the time, Pallas kernels for 0%

commit v1 on v0

--- a/solution.py
+++ b/solution.py
@@ -1,24 +1,329 @@
+import functools
+
 import jax
 import jax.numpy as jnp
 from jax import lax
+from jax.experimental import pallas as pl
+from jax.experimental.pallas import tpu as pltpu
 from jax.sharding import PartitionSpec as P
 
 HEADS = 8
 HEAD_DIM = 128
 WIDTH = 5
-
-
-def with_halo(block, sides, width):
-    for axis, dim in sides:
-        count = lax.axis_size(axis)
-        forward = [(i, i + 1) for i in range(count - 1)]
-        backward = [(target, source) for source, target in forward]
-        low = lax.ppermute(
-            lax.slice_in_dim(block, block.shape[dim] - width, None, axis=dim), axis, forward
-        )
-        high = lax.ppermute(lax.slice_in_dim(block, 0, width, axis=dim), axis, backward)
-        block = jnp.concatenate([low, block, high], axis=dim)
-    return block
+MESH = pl.DeviceIdType.MESH
+HALO = 16
+MB = 1024 * 1024
+
+
+def conv_kernel(count, seq_ref, w_ref, pooled_ref, low, high, wbuf, ebuf, obuf, taps, send_sem, recv_sem, w_sem):
+    me = lax.axis_index("seq")
+    half, wide = seq_ref.shape
+    d = wide // 2
+    step = wbuf.shape[2]
+    chunks = d // step
+    has_low = me > 0
+    has_high = me < count - 1
+    low_id = {"seq": lax.rem(me + count - 1, count)}
+    high_id = {"seq": lax.rem(me + 1, count)}
+
+    def w_copy(c):
+        return pltpu.make_async_copy(w_ref.at[:, pl.ds(c * step, step)], wbuf.at[c], w_sem.at[c])
+
+    for c in range(chunks):
+        w_copy(c).start()
+
+    barrier = pltpu.get_barrier_semaphore()
+
+    for peer in (low_id, high_id):
+        pl.semaphore_signal(barrier, inc=1, device_id=peer, device_id_type=MESH)
+    pl.semaphore_wait(barrier, 2)
+
+    up = pltpu.make_async_remote_copy(
+        src_ref=seq_ref.at[pl.ds(half - HALO, HALO)], dst_ref=low,
+        send_sem=send_sem.at[0], recv_sem=recv_sem.at[0], device_id=high_id, device_id_type=MESH)
+    down = pltpu.make_async_remote_copy(
+        src_ref=seq_ref.at[pl.ds(0, HALO)], dst_ref=high,
+        send_sem=send_sem.at[1], recv_sem=recv_sem.at[1], device_id=low_id, device_id_type=MESH)
+
+    @pl.when(has_high)
+    def _():
+        up.start()
+
+    @pl.when(has_low)
+    def _():
+        down.start()
+
+    def activate(rows):
+        rows = rows.astype(jnp.float32)
+        scale = lax.rsqrt(jnp.mean(rows * rows, axis=-1, keepdims=True) + 1e-06)
+        return jax.nn.gelu(rows * scale)
+
+    block = 32
+
+    def act_step(i, _):
+        r = pl.multiple_of(i * block, block)
+        ebuf[pl.ds(r + 8, block), :] = activate(seq_ref[pl.ds(r, block), :d])
+        obuf[pl.ds(r + 8, block), :] = activate(seq_ref[pl.ds(r, block), d:])
+        return 0
+
+    lax.fori_loop(0, half // block, act_step, 0)
+
+    @pl.when(has_low)
+    def _():
+        down.wait_send()
+        up.wait_recv()
+        ebuf[0:8, :] = activate(low[:, :d])[8:16]
+        obuf[0:8, :] = activate(low[:, d:])[8:16]
+
+    @pl.when(jnp.logical_not(has_low))
+    def _():
+        ebuf[0:8, :] = jnp.zeros((8, d), jnp.float32)
+        obuf[0:8, :] = jnp.zeros((8, d), jnp.float32)
+
+    @pl.when(has_high)
+    def _():
+        up.wait_send()
+        down.wait_recv()
+        ebuf[half + 8 : half + 16, :] = activate(high[:, :d])[0:8]
+        obuf[half + 8 : half + 16, :] = activate(high[:, d:])[0:8]
+
+    @pl.when(jnp.logical_not(has_high))
+    def _():
+        ebuf[half + 8 : half + 16, :] = jnp.zeros((8, d), jnp.float32)
+        obuf[half + 8 : half + 16, :] = jnp.zeros((8, d), jnp.float32)
+
+    def place(c, _):
+        k = pl.multiple_of(c * step, step)
+        cols = pl.ds(k, step)
+
+        def put(first, tap, value):
+            taps[first : first + half, pl.ds(tap * d + k, step)] = value
+
+        e_prev = ebuf[7 : 7 + half, cols].astype(jnp.bfloat16)
+        e_here = ebuf[8 : 8 + half, cols].astype(jnp.bfloat16)
+        e_next = ebuf[9 : 9 + half, cols].astype(jnp.bfloat16)
+        put(0, 0, e_prev)
+        put(0, 2, e_here)
+        put(half, 1, e_here)
+        put(0, 4, e_next)
+        put(half, 3, e_next)
+        o_prev = obuf[7 : 7 + half, cols].astype(jnp.bfloat16)
+        o_here = obuf[8 : 8 + half, cols].astype(jnp.bfloat16)
+        o_next = obuf[9 : 9 + half, cols].astype(jnp.bfloat16)
+        put(0, 1, o_prev)
+        put(half, 0, o_prev)
+        put(0, 3, o_here)
+        put(half, 2, o_here)
+        put(half, 4, o_next)
+        return 0
+
+    lax.fori_loop(0, chunks, place, 0)
+
+    def conv_step(c, _):
+        w_copy(c).wait()
+        k = pl.multiple_of(c * step, step)
+        mixed = jnp.dot(taps[...], wbuf[c], preferred_element_type=jnp.float32)
+        even = mixed[:half] + seq_ref[:, pl.ds(k, step)].astype(jnp.float32)
+        odd = mixed[half:] + seq_ref[:, pl.ds(k + d, step)].astype(jnp.float32)
+        pooled_ref[:, pl.ds(k, step)] = jnp.maximum(even, odd).astype(jnp.bfloat16)
+        return 0
+
+    lax.fori_loop(0, chunks, conv_step, 0)
+
+
+def conv_pool(sequence, conv_weight, count):
+    rows, d = sequence.shape
+    half = rows // 2
+    step = 256
+    pairs = sequence.reshape(half, 2 * d)
+    weight = conv_weight.reshape(WIDTH * d, d)
+    return pl.pallas_call(
+        functools.partial(conv_kernel, count),
+        out_shape=jax.ShapeDtypeStruct((half, d), jnp.bfloat16),
+        in_specs=[pl.BlockSpec(memory_space=pltpu.VMEM), pl.BlockSpec(memory_space=pl.ANY)],
+        out_specs=pl.BlockSpec(memory_space=pltpu.VMEM),
+        scratch_shapes=[
+            pltpu.VMEM((HALO, 2 * d), jnp.bfloat16),
+            pltpu.VMEM((HALO, 2 * d), jnp.bfloat16),
+            pltpu.VMEM((d // step, WIDTH * d, step), jnp.bfloat16),
+            pltpu.VMEM((half + 16, d), jnp.float32),
+            pltpu.VMEM((half + 16, d), jnp.float32),
+            pltpu.VMEM((rows, WIDTH * d), jnp.bfloat16),
+            pltpu.SemaphoreType.DMA((2,)),
+            pltpu.SemaphoreType.DMA((2,)),
+            pltpu.SemaphoreType.DMA((d // step,)),
+        ],
+        compiler_params=pltpu.CompilerParams(
+            collective_id=0, has_side_effects=True, vmem_limit_bytes=52 * MB),
+        cost_estimate=pl.CostEstimate(
+            flops=2 * rows * WIDTH * d * d, bytes_accessed=2 * WIDTH * d * d, transcendentals=rows * d),
+        name="conv_pool",
+    )(pairs, weight)
+
+
+def attend_kernel(pooled_ref, w_ref, out_w_ref, update_ref, normed, wbuf, owbuf, send, recv, att_send, att_recv,
+                  send_sem, recv_sem, asend_sem, arecv_sem, w_sem):
+    me = lax.axis_index("seq")
+    count, d = pooled_ref.shape
+    inner = HEADS * HEAD_DIM
+
+    def w_copy(t):
+        return pltpu.make_async_copy(w_ref.at[:, pl.ds(t * inner, inner)], wbuf.at[t], w_sem.at[t])
+
+    order = (1, 2, 0)
+    for t in order:
+        w_copy(t).start()
+    ow_copy = pltpu.make_async_copy(out_w_ref, owbuf, w_sem.at[3])
+    ow_copy.start()
+
+    barrier = pltpu.get_barrier_semaphore()
+
+    def greet(o, _):
+        pl.semaphore_signal(
+            barrier, inc=1, device_id={"seq": lax.rem(me + o, HEADS)}, device_id_type=MESH)
+        return 0
+
+    lax.fori_loop(1, HEADS, greet, 0)
+
+    def norm_step(i, _):
+        r = pl.multiple_of(i * 32, 32)
+        rows = pooled_ref[pl.ds(r, 32), :].astype(jnp.float32)
+        scale = lax.rsqrt(jnp.mean(rows * rows, axis=-1, keepdims=True) + 1e-06)
+        normed[pl.ds(r, 32), :] = (rows * scale).astype(jnp.bfloat16)
+        return 0
+
+    lax.fori_loop(0, count // 32, norm_step, 0)
+    pl.semaphore_wait(barrier, HEADS - 1)
+
+    def piece(t, peer, slot):
+        return pltpu.make_async_remote_copy(
+            src_ref=send.at[t, peer], dst_ref=recv.at[t, slot],
+            send_sem=send_sem.at[t, peer], recv_sem=recv_sem.at[t, slot],
+            device_id={"seq": peer}, device_id_type=MESH)
+
+    def back(peer, slot):
+        return pltpu.make_async_remote_copy(
+            src_ref=att_send.at[peer], dst_ref=att_recv.at[slot],
+            send_sem=asend_sem.at[peer], recv_sem=arecv_sem.at[slot],
+            device_id={"seq": peer}, device_id_type=MESH)
+
+    for t in order:
+        w_copy(t).wait()
+
+        def project(p, _, t=t):
+            k = pl.multiple_of(p * 256, 256)
+            both = jnp.dot(
+                normed[...], wbuf[t, :, pl.ds(k, 256)], preferred_element_type=jnp.float32
+            ).astype(jnp.bfloat16)
+            send[t, 2 * p] = both[:, :HEAD_DIM]
+            send[t, 2 * p + 1] = both[:, HEAD_DIM:]
+            return 0
+
+        lax.fori_loop(0, HEADS // 2, project, 0)
+
+        def post(o, _, t=t):
+            piece(t, lax.rem(me + o, HEADS), me).start()
+            return 0
+
+        lax.fori_loop(1, HEADS, post, 0)
+        recv[t, me] = send[t, me]
+
+    def arrive(t):
+        def one(o, _):
+            source = lax.rem(me + HEADS - o, HEADS)
+            piece(t, source, source).wait_recv()
+            return 0
+
+        lax.fori_loop(1, HEADS, one, 0)
+
+    arrive(1)
+    arrive(2)
+    keys = recv.at[1]
+    values = recv.at[2]
+    factor = HEAD_DIM ** (-0.5) * 1.4426950408889634
+
+    def attend(source):
+        total_rows = HEADS * count
+        raw = lax.dot_general(
+            recv[0, source], keys[...].reshape(total_rows, HEAD_DIM),
+            (((1,), (1,)), ((), ())), preferred_element_type=jnp.float32)
+        peak = jnp.max(raw, axis=-1, keepdims=True)
+        expo = jnp.exp2((raw - peak) * factor)
+        total = jnp.sum(expo, axis=-1, keepdims=True)
+        weighted = jnp.dot(
+            expo.astype(jnp.bfloat16), values[...].reshape(total_rows, HEAD_DIM),
+            preferred_element_type=jnp.float32)
+        return (weighted / total).astype(jnp.bfloat16)
+
+    def step(o, _):
+        source = lax.rem(me + HEADS - o, HEADS)
+
+        @pl.when(o > 0)
+        def _():
+            piece(0, source, source).wait_recv()
+
+        att_send[source] = attend(source)
+
+        @pl.when(o > 0)
+        def _():
+            back(source, me).start()
+
+        return 0
+
+    lax.fori_loop(0, HEADS, step, 0)
+    att_recv[me] = att_send[me]
+
+    def finish(o, _):
+        peer = lax.rem(me + o, HEADS)
+        for t in range(3):
+            piece(t, peer, me).wait_send()
+        back(peer, me).wait_send()
+        back(peer, peer).wait_recv()
+        return 0
+
+    lax.fori_loop(1, HEADS, finish, 0)
+    ow_copy.wait()
+    joined = jnp.concatenate([att_recv[h] for h in range(HEADS)], axis=1)
+    for p in range(d // 512):
+        update_ref[:, p * 512 : (p + 1) * 512] = jnp.dot(
+            joined, owbuf[:, p * 512 : (p + 1) * 512], preferred_element_type=jnp.float32
+        ).astype(jnp.bfloat16)
+
+
+def attention(pooled, qkv, out_weight):
+    count, d = pooled.shape
+    inner = HEADS * HEAD_DIM
+    heads = (HEADS, count, HEAD_DIM)
+    return pl.pallas_call(
+        attend_kernel,
+        out_shape=jax.ShapeDtypeStruct((count, d), jnp.bfloat16),
+        in_specs=[
+            pl.BlockSpec(memory_space=pltpu.VMEM),
+            pl.BlockSpec(memory_space=pl.ANY),
+            pl.BlockSpec(memory_space=pl.ANY),
+        ],
+        out_specs=pl.BlockSpec(memory_space=pltpu.VMEM),
+        scratch_shapes=[
+            pltpu.VMEM((count, d), jnp.bfloat16),
+            pltpu.VMEM((3, d, inner), jnp.bfloat16),
+            pltpu.VMEM((inner, d), jnp.bfloat16),
+            pltpu.VMEM((3,) + heads, jnp.bfloat16),
+            pltpu.VMEM((3,) + heads, jnp.bfloat16),
+            pltpu.VMEM(heads, jnp.bfloat16),
+            pltpu.VMEM(heads, jnp.bfloat16),
+            pltpu.SemaphoreType.DMA((3, HEADS)),
+            pltpu.SemaphoreType.DMA((3, HEADS)),
+            pltpu.SemaphoreType.DMA((HEADS,)),
+            pltpu.SemaphoreType.DMA((HEADS,)),
+            pltpu.SemaphoreType.DMA((4,)),
+        ],
+        compiler_params=pltpu.CompilerParams(
+            collective_id=1, has_side_effects=True, vmem_limit_bytes=44 * MB),
+        cost_estimate=pl.CostEstimate(
+            flops=2 * count * d * 4 * inner + 4 * count * HEADS * count * inner,
+            bytes_accessed=8 * d * inner, transcendentals=count * count * HEADS * HEADS),
+        name="attend",
+    )(pooled, qkv, out_weight)
 
 
 def normalize(values):
@@ -38,24 +343,12 @@
     ).astype(jnp.bfloat16)
 
 
-def on_device(sequence, conv_weight, qkv_weight, out_weight):
-    length = sequence.shape[0]
+def attention_groups(pooled, qkv_weight, out_weight):
     inner = HEADS * HEAD_DIM
-    extended = with_halo(sequence, (("seq", 0),), 2)
-    activated = jax.nn.gelu(normalize(extended.astype(jnp.float32))).astype(jnp.bfloat16)
-    mixed = sequence.astype(jnp.float32)
-    for offset in range(WIDTH):
-        mixed = mixed + jnp.dot(
-            activated[offset : offset + length],
-            conv_weight[offset],
-            preferred_element_type=jnp.float32,
-        )
-    pooled = jnp.max(mixed.reshape(length // 2, 2, -1), axis=1).astype(jnp.bfloat16)
     count = pooled.shape[0]
     normed = normalize(pooled.astype(jnp.float32)).astype(jnp.bfloat16)
-    columns = normed
     projected = jnp.dot(
-        columns,
+        normed,
         lax.all_gather(qkv_weight, "seq", axis=0, tiled=True),
         preferred_element_type=jnp.float32,
     ).astype(jnp.bfloat16)
@@ -96,7 +389,21 @@
         lax.all_gather(out_weight, "seq", axis=0, tiled=True),
         preferred_element_type=jnp.float32,
     )
-    return (pooled, update.astype(jnp.bfloat16))
+    return update.astype(jnp.bfloat16)
+
+
+def on_device(sequence, conv_weight, qkv_weight, out_weight):
+    count = lax.axis_size("seq")
+    pooled = conv_pool(sequence, conv_weight, count)
+    if count == HEADS:
+        update = attention(
+            pooled,
+            lax.all_gather(qkv_weight, "seq", axis=0, tiled=True),
+            lax.all_gather(out_weight, "seq", axis=0, tiled=True),
+        )
+    else:
+        update = attention_groups(pooled, qkv_weight, out_weight)
+    return (pooled, update)
 
 
 def solution(mesh):

time: 209 us -> 208 us (level)
  Pallas kernels: 0 us -> 77.7 us
  matrix products: 42.3 us -> 0 us
  starting transfers between devices: 14.4 us -> 0.08 us
  other arithmetic: 12.7 us -> 0 us
  local copies, waits for them, and re-layouts: 13 us -> 7.24 us
  waiting for transfers between devices: 112 us -> 109 us
    pallas_call x0 -> x2, Pallas kernels: none -> 77.7 us  [the longest x1 55.1 us: attention(): pl.pallas_call(attend_kernel, out_shape=jax.ShapeDtypeStruct((count, d),...]
    all_to_all x3 -> x0, waiting for transfers between devices: 48.5 us -> none  [the longest x1 24.5 us: on_device(): lax.all_to_all(pair_send, 'seq', split_axis=0, concat_axis=0, tiled=True)]
    dot_general x23 -> x0, matrix products: 42.3 us -> none  [the longest x5 23.8 us: on_device(): jnp.dot(activated[offset:offset + length], conv_weight[offset], preferred...]
    all_gather x1, waiting for transfers between devices: 53 us -> 91.3 us  [on_device(): lax.all_gather(qkv_weight, 'seq', axis=0, tiled=True)]
    all_to_all x3 -> x0, starting transfers between devices: 10.7 us -> none  [the longest x1 3.63 us: on_device(): lax.all_to_all(head_rows, 'seq', split_axis=0, concat_axis=0, tiled=True)]
    all_gather x1, waiting for transfers between devices: 5.28 us -> 15.9 us  [on_device(): lax.all_gather(out_weight, 'seq', axis=0, tiled=True)]
    dynamic_update_slice x16 -> x0, local copies, waits for them, and re-layouts: 5.97 us -> none  [on_device(): head_rows = lax.map(per_source, query_recv)]
    reduce_sum x10 -> x0, other arithmetic: 5.76 us -> none  [the longest x8 3.51 us: single_head(): total = jnp.sum(expo, axis=-1, keepdims=True)]
  transfers between devices with their start and end apart: 7 -> 2, of which waited for: 6 -> 2; matrix products, arithmetic and copies ran while one was open for 26% -> 2% of each run, Pallas kernels for 0% -> 11%
where the time goes in v1:
time: 208 us
  waiting for transfers between devices  109 us (52%)
  Pallas kernels  77.7 us (37%)
  between operations  14.1 us (7%)
  local copies, waits for them, and re-layouts  7.24 us (3%)
    all_gather x1, waiting for transfers between devices, on_device(): lax.all_gather(qkv_weight, 'seq', axis=0, tiled=True)  91.3 us
    pallas_call x1, Pallas kernels, attention(): pl.pallas_call(attend_kernel, out_shape=jax.ShapeDtypeStruct((count, d),...  55.1 us
    pallas_call x1, Pallas kernels, conv_pool(): pl.pallas_call(functools.partial(conv_kernel, count), out_shape=jax.Shape...  22.5 us
    all_gather x1, waiting for transfers between devices, on_device(): lax.all_gather(out_weight, 'seq', axis=0, tiled=True)  15.9 us
  transfers between devices with their start and end apart: 2, of which 2 were waited for; matrix products, arithmetic and copies ran while one was open for 2% of the time, Pallas kernels for 11%

profile of v1, /device:TPU:0, one launch (start us, length us, event | category | flops | bytes accessed | tf_op | source)
XLA Modules:
  0.0 207.6 jit_solution(7043471474799494298)
XLA Ops:
  7.2 0.0 all-gather.5.cloned.1.call-start
  7.2 0.7 all-gather.5.cloned.1.call-update
  7.9 0.0 all-gather.3.cloned.1.call-start
  7.9 0.7 all-gather.3.cloned.1.call-update
  8.6 3.6 %reshape.10.seq_ref = bf16[256,3072]{1,0:T(8,128)(2,1)} reshape(bf16[512,1536]{1,0:T(8,128)(2,1)} %param.4) | data formatting | bytes 3145728 | tf_op jit(solution)/shard_map/reshape | solution.py:138
  12.2 22.5 %conv_pool.1.pooled_ref = bf16[256,1536]{1,0:T(8,128)(2,1)S(1)} custom-call(bf16[256,3072]{1,0:T(8,128)(2,1)} %reshape.10.seq_ref, bf16[7680,1536]{1,0:T(8,128)(2,1)} %bitcast.1), custom_call_target="tpu_custom_call" | custom-call | flops 12079595520 | bytes 23592960 | tf_op jit(solution)/shard_map/conv_pool/pallas_call | solution.py:140
  34.8 15.9 %all-gather.5.cloned.1.call-done.out_w_ref = bf16[1024,1536]{1,0:T(8,128)(2,1)} async-done(((bf16[128,1536]{1,0:T(8,128)(2,1)}), bf16[1024,1536]{1,0:T(8,128)(2,1)}) %all-gather.5.cloned.1.call-update) | async-done | bytes 3145744 | tf_op jit(solution)/shard_map/all_gather | solution.py:402
  50.7 91.3 %all-gather.3.cloned.1.call-done.w_ref = bf16[1536,3072]{1,0:T(8,128)(2,1)} async-done(((bf16[192,3072]{1,0:T(8,128)(2,1)}), bf16[1536,3072]{1,0:T(8,128)(2,1)}) %all-gather.3.cloned.1.call-update) | async-done | bytes 9437200 | tf_op jit(solution)/shard_map/all_gather | solution.py:401
  141.9 0.0 copy-start
  141.9 1.9 copy-done
  143.8 55.1 %attend.1 = bf16[256,1536]{1,0:T(8,128)(2,1)S(1)} custom-call(bf16[256,1536]{1,0:T(8,128)(2,1)S(1)} %conv_pool.1.pooled_ref, bf16[1536,3072]{1,0:T(8,128)(2,1)} %all-gather.3.cloned.1.call-done.w_ref, bf16[1024,1536]{1,0:T(8,128)(2,1)S(1)} %copy-done), custom_call_target="tpu_custom_call" | custom-call | flops 5368709120 | bytes 12582912 | tf_op jit(solution)/shard_map/attend/pallas_call | solution.py:297
  199.0 0.9 copy.8
  199.9 0.9 copy.9
Async XLA Ops:
  7.2 43.5 %all-gather.5.cloned.1.call-start = ((), (), s32[]{:S(2)}) async-start(), calls=%async_computation.1 | async-start | bytes 3538944 | tf_op jit(solution)/shard_map/all_gather | solution.py:402
  7.9 134.0 %all-gather.3.cloned.1.call-start = ((), (), s32[]{:S(2)}) async-start(), calls=%async_computation | async-start | bytes 10616832 | tf_op jit(solution)/shard_map/all_gather | solution.py:401
  141.9 1.9 copy-start
Sparse Core Ops, SparseCore 0:
  9.6 40.9 all-gather.4
  52.3 89.5 all-gather.2

commit v2 on v1

--- a/solution.py
+++ b/solution.py
@@ -13,9 +13,133 @@
 MESH = pl.DeviceIdType.MESH
 HALO = 16
 MB = 1024 * 1024
-
-
-def conv_kernel(count, seq_ref, w_ref, pooled_ref, low, high, wbuf, ebuf, obuf, taps, send_sem, recv_sem, w_sem):
+DP = 4
+PAIRS = 4
+REMOTE = 6
+
+
+class Gather:
+    def __init__(self, shard, whole, sems):
+        self.shard, self.whole = shard, whole
+        self.s1, self.r1, self.s2, self.r2, self.s3, self.r3, self.own_sem = sems
+        self.me = lax.axis_index("seq")
+        self.dp = lax.axis_index("dp")
+        self.pair, self.core = self.me // 2, self.me % 2
+        self.mate = self.pair * 2 + 1 - self.core
+        self.width = whole.shape[2] // (2 * DP)
+
+    def part(self, source, group, core):
+        first = pl.multiple_of((2 * group + core) * self.width, 128)
+        return self.whole.at[source, :, pl.ds(first, self.width)]
+
+    def own(self):
+        return pltpu.make_async_copy(self.shard, self.whole.at[self.me], self.own_sem.at[0])
+
+    def to_mate(self):
+        return pltpu.make_async_remote_copy(
+            src_ref=self.shard, dst_ref=self.whole.at[self.me], send_sem=self.s1.at[self.mate],
+            recv_sem=self.r1.at[self.me], device_id={"seq": self.mate}, device_id_type=MESH)
+
+    def from_mate(self):
+        return pltpu.make_async_remote_copy(
+            src_ref=self.shard, dst_ref=self.whole.at[self.mate], send_sem=self.s1.at[self.me],
+            recv_sem=self.r1.at[self.mate], device_id={"seq": self.mate}, device_id_type=MESH)
+
+    def target(self, i):
+        return ((self.pair + PAIRS - 1 - i // 2) % PAIRS) * 2 + i % 2
+
+    def source(self, i):
+        return ((self.pair + 1 + i // 2) % PAIRS) * 2 + i % 2
+
+    def out1(self, i):
+        peer = self.target(i)
+        first = pl.multiple_of((2 * self.dp + peer % 2) * self.width, 128)
+        return pltpu.make_async_remote_copy(
+            src_ref=self.shard.at[:, pl.ds(first, self.width)], dst_ref=self.part(self.me, self.dp, peer % 2),
+            send_sem=self.s1.at[peer], recv_sem=self.r1.at[self.me], device_id={"seq": peer}, device_id_type=MESH)
+
+    def in1(self, i):
+        source = self.source(i)
+        block = self.part(source, self.dp, self.core)
+        return pltpu.make_async_remote_copy(
+            src_ref=block, dst_ref=block, send_sem=self.s1.at[source], recv_sem=self.r1.at[source],
+            device_id={"seq": source}, device_id_type=MESH)
+
+    def out2(self, i, j):
+        source, peer = self.source(i), (self.dp + j) % DP
+        block = self.part(source, self.dp, self.core)
+        return pltpu.make_async_remote_copy(
+            src_ref=block, dst_ref=block, send_sem=self.s2.at[source, peer], recv_sem=self.r2.at[source, self.dp],
+            device_id={"dp": peer}, device_id_type=MESH)
+
+    def in2(self, i, j):
+        source, peer = self.source(i), (self.dp + j) % DP
+        block = self.part(source, peer, self.core)
+        return pltpu.make_async_remote_copy(
+            src_ref=block, dst_ref=block, send_sem=self.s2.at[source, peer], recv_sem=self.r2.at[source, peer],
+            device_id={"dp": peer}, device_id_type=MESH)
+
+    def out3(self, i, group):
+        source = self.source(i)
+        block = self.part(source, group, self.core)
+        return pltpu.make_async_remote_copy(
+            src_ref=block, dst_ref=block, send_sem=self.s3.at[source, group], recv_sem=self.r3.at[source, group],
+            device_id={"seq": self.mate}, device_id_type=MESH)
+
+    def in3(self, i, group):
+        source = self.source(i)
+        block = self.part(source, group, 1 - self.core)
+        return pltpu.make_async_remote_copy(
+            src_ref=block, dst_ref=block, send_sem=self.s3.at[source, group], recv_sem=self.r3.at[source, group],
+            device_id={"seq": self.mate}, device_id_type=MESH)
+
+    def start(self):
+        self.own().start()
+        self.to_mate().start()
+
+        def one(i, _):
+            self.out1(i).start()
+            return 0
+
+        lax.fori_loop(0, REMOTE, one, 0)
+
+    def relay(self, i):
+        self.in1(i).wait_recv()
+        for j in range(1, DP):
+            self.out2(i, j).start()
+        self.out3(i, self.dp).start()
+
+    def finish(self):
+        def second(i, _):
+            for j in range(1, DP):
+                self.in2(i, j).wait_recv()
+                self.out3(i, (self.dp + j) % DP).start()
+            return 0
+
+        lax.fori_loop(0, REMOTE, second, 0)
+
+        def last(i, _):
+            self.out1(i).wait_send()
+            for j in range(1, DP):
+                self.out2(i, j).wait_send()
+            for group in range(DP):
+                self.out3(i, group).wait_send()
+                self.in3(i, group).wait_recv()
+            return 0
+
+        lax.fori_loop(0, REMOTE, last, 0)
+        self.own().wait()
+        self.to_mate().wait_send()
+        self.from_mate().wait_recv()
+
+
+def conv_kernel(count, share, *refs):
+    if share:
+        seq_ref, w_ref, shard, pooled_ref, whole, *refs = refs
+    else:
+        seq_ref, w_ref, pooled_ref, *refs = refs
+    low, high, wbuf, ebuf, obuf, taps, send_sem, recv_sem, w_sem, *sems = refs
+    gather = Gather(shard, whole, sems) if share else None
     me = lax.axis_index("seq")
     half, wide = seq_ref.shape
     d = wide // 2
@@ -34,9 +158,18 @@
 
     barrier = pltpu.get_barrier_semaphore()
 
-    for peer in (low_id, high_id):
-        pl.semaphore_signal(barrier, inc=1, device_id=peer, device_id_type=MESH)
-    pl.semaphore_wait(barrier, 2)
+    if share:
+        for o in range(1, count):
+            pl.semaphore_signal(
+                barrier, inc=1, device_id={"seq": lax.rem(me + o, count)}, device_id_type=MESH)
+        for o in range(1, DP):
+            pl.semaphore_signal(
+                barrier, inc=1, device_id={"dp": (gather.dp + o) % DP}, device_id_type=MESH)
+        pl.semaphore_wait(barrier, count + DP - 2)
+    else:
+        for peer in (low_id, high_id):
+            pl.semaphore_signal(barrier, inc=1, device_id=peer, device_id_type=MESH)
+        pl.semaphore_wait(barrier, 2)
 
     up = pltpu.make_async_remote_copy(
         src_ref=seq_ref.at[pl.ds(half - HALO, HALO)], dst_ref=low,
@@ -52,6 +185,9 @@
     @pl.when(has_low)
     def _():
         down.start()
+
+    if share:
+        gather.start()
 
     def activate(rows):
         rows = rows.astype(jnp.float32)
@@ -126,22 +262,38 @@
         even = mixed[:half] + seq_ref[:, pl.ds(k, step)].astype(jnp.float32)
         odd = mixed[half:] + seq_ref[:, pl.ds(k + d, step)].astype(jnp.float32)
         pooled_ref[:, pl.ds(k, step)] = jnp.maximum(even, odd).astype(jnp.bfloat16)
+        if share:
+            gather.relay(c)
         return 0
 
     lax.fori_loop(0, chunks, conv_step, 0)
-
-
-def conv_pool(sequence, conv_weight, count):
+    if share:
+        gather.finish()
+
+
+def conv_pool(sequence, conv_weight, count, shard=None):
     rows, d = sequence.shape
     half = rows // 2
     step = 256
     pairs = sequence.reshape(half, 2 * d)
     weight = conv_weight.reshape(WIDTH * d, d)
+    share = shard is not None
+    out_shape = jax.ShapeDtypeStruct((half, d), jnp.bfloat16)
+    out_specs = pl.BlockSpec(memory_space=pltpu.VMEM)
+    in_specs = [pl.BlockSpec(memory_space=pltpu.VMEM), pl.BlockSpec(memory_space=pl.ANY)]
+    operands, sems = [pairs, weight], []
+    if share:
+        out_shape = (out_shape, jax.ShapeDtypeStruct((count,) + shard.shape, jnp.bfloat16))
+        out_specs = (out_specs, pl.BlockSpec(memory_space=pl.ANY))
+        in_specs.append(pl.BlockSpec(memory_space=pl.ANY))
+        operands.append(shard)
+        sems = [pltpu.SemaphoreType.DMA((count,))] * 2 + [pltpu.SemaphoreType.DMA((count, DP))] * 4
+        sems.append(pltpu.SemaphoreType.DMA((1,)))
     return pl.pallas_call(
-        functools.partial(conv_kernel, count),
-        out_shape=jax.ShapeDtypeStruct((half, d), jnp.bfloat16),
-        in_specs=[pl.BlockSpec(memory_space=pltpu.VMEM), pl.BlockSpec(memory_space=pl.ANY)],
-        out_specs=pl.BlockSpec(memory_space=pltpu.VMEM),
+        functools.partial(conv_kernel, count, share),
+        out_shape=out_shape,
+        in_specs=in_specs,
+        out_specs=out_specs,
         scratch_shapes=[
             pltpu.VMEM((HALO, 2 * d), jnp.bfloat16),
             pltpu.VMEM((HALO, 2 * d), jnp.bfloat16),
@@ -152,29 +304,35 @@
             pltpu.SemaphoreType.DMA((2,)),
             pltpu.SemaphoreType.DMA((2,)),
             pltpu.SemaphoreType.DMA((d // step,)),
-        ],
+        ] + sems,
         compiler_params=pltpu.CompilerParams(
             collective_id=0, has_side_effects=True, vmem_limit_bytes=52 * MB),
         cost_estimate=pl.CostEstimate(
             flops=2 * rows * WIDTH * d * d, bytes_accessed=2 * WIDTH * d * d, transcendentals=rows * d),
         name="conv_pool",
-    )(pairs, weight)
-
-
-def attend_kernel(pooled_ref, w_ref, out_w_ref, update_ref, normed, wbuf, owbuf, send, recv, att_send, att_recv,
+    )(*operands)
+
+
+def attend_kernel(pooled_ref, w_ref, update_ref, normed, wbuf, owbuf, send, recv, att_send, att_recv,
                   send_sem, recv_sem, asend_sem, arecv_sem, w_sem):
     me = lax.axis_index("seq")
     count, d = pooled_ref.shape
     inner = HEADS * HEAD_DIM
+    depth = d // HEADS
 
     def w_copy(t):
-        return pltpu.make_async_copy(w_ref.at[:, pl.ds(t * inner, inner)], wbuf.at[t], w_sem.at[t])
+        return pltpu.make_async_copy(
+            w_ref.at[:, pl.ds(0, depth), pl.ds(t * inner, inner)], wbuf.at[t], w_sem.at[t])
+
+    def ow_copy(part):
+        return pltpu.make_async_copy(
+            w_ref.at[:, pl.ds(depth, HEAD_DIM // 2), pl.ds(part * d, d)], owbuf.at[:, part], w_sem.at[3 + part])
 
     order = (1, 2, 0)
     for t in order:
         w_copy(t).start()
-    ow_copy = pltpu.make_async_copy(out_w_ref, owbuf, w_sem.at[3])
-    ow_copy.start()
+    for part in range(2):
+        ow_copy(part).start()
 
     barrier = pltpu.get_barrier_semaphore()
 
@@ -213,7 +371,7 @@
         def project(p, _, t=t):
             k = pl.multiple_of(p * 256, 256)
             both = jnp.dot(
-                normed[...], wbuf[t, :, pl.ds(k, 256)], preferred_element_type=jnp.float32
+                normed[...], wbuf[t, :, :, pl.ds(k, 256)].reshape(d, 256), preferred_element_type=jnp.float32
             ).astype(jnp.bfloat16)
             send[t, 2 * p] = both[:, :HEAD_DIM]
             send[t, 2 * p + 1] = both[:, HEAD_DIM:]
@@ -282,15 +440,16 @@
         return 0
 
     lax.fori_loop(1, HEADS, finish, 0)
-    ow_copy.wait()
+    for part in range(2):
+        ow_copy(part).wait()
     joined = jnp.concatenate([att_recv[h] for h in range(HEADS)], axis=1)
     for p in range(d // 512):
         update_ref[:, p * 512 : (p + 1) * 512] = jnp.dot(
-            joined, owbuf[:, p * 512 : (p + 1) * 512], preferred_element_type=jnp.float32
+            joined, owbuf[:, :, :, p * 512 : (p + 1) * 512].reshape(inner, 512), preferred_element_type=jnp.float32
         ).astype(jnp.bfloat16)
 
 
-def attention(pooled, qkv, out_weight):
+def attention(pooled, weights):
     count, d = pooled.shape
     inner = HEADS * HEAD_DIM
     heads = (HEADS, count, HEAD_DIM)
@@ -300,13 +459,12 @@
         in_specs=[
             pl.BlockSpec(memory_space=pltpu.VMEM),
             pl.BlockSpec(memory_space=pl.ANY),
-            pl.BlockSpec(memory_space=pl.ANY),
         ],
         out_specs=pl.BlockSpec(memory_space=pltpu.VMEM),
         scratch_shapes=[
             pltpu.VMEM((count, d), jnp.bfloat16),
-            pltpu.VMEM((3, d, inner), jnp.bfloat16),
-            pltpu.VMEM((inner, d), jnp.bfloat16),
+            pltpu.VMEM((3, HEADS, d // HEADS, inner), jnp.bfloat16),
+            pltpu.VMEM((HEADS, 2, HEAD_DIM // 2, d), jnp.bfloat16),
             pltpu.VMEM((3,) + heads, jnp.bfloat16),
             pltpu.VMEM((3,) + heads, jnp.bfloat16),
             pltpu.VMEM(heads, jnp.bfloat16),
@@ -315,7 +473,7 @@
             pltpu.SemaphoreType.DMA((3, HEADS)),
             pltpu.SemaphoreType.DMA((HEADS,)),
             pltpu.SemaphoreType.DMA((HEADS,)),
-            pltpu.SemaphoreType.DMA((4,)),
+            pltpu.SemaphoreType.DMA((5,)),
         ],
         compiler_params=pltpu.CompilerParams(
             collective_id=1, has_side_effects=True, vmem_limit_bytes=44 * MB),
@@ -323,7 +481,7 @@
             flops=2 * count * d * 4 * inner + 4 * count * HEADS * count * inner,
             bytes_accessed=8 * d * inner, transcendentals=count * count * HEADS * HEADS),
         name="attend",
-    )(pooled, qkv, out_weight)
+    )(pooled, weights)
 
 
 def normalize(values):
@@ -394,14 +552,14 @@
 
 def on_device(sequence, conv_weight, qkv_weight, out_weight):
     count = lax.axis_size("seq")
-    pooled = conv_pool(sequence, conv_weight, count)
-    if count == HEADS:
-        update = attention(
-            pooled,
-            lax.all_gather(qkv_weight, "seq", axis=0, tiled=True),
-            lax.all_gather(out_weight, "seq", axis=0, tiled=True),
-        )
+    if count == HEADS and lax.axis_size("dp") == DP:
+        part = out_weight.shape[0] // 2
+        shard = jnp.concatenate(
+            [qkv_weight, jnp.concatenate([out_weight[:part], out_weight[part:]], axis=1)], axis=0)
+        pooled, weights = conv_pool(sequence, conv_weight, count, shard)
+        update = attention(pooled, weights)
     else:
+        pooled = conv_pool(sequence, conv_weight, count)
         update = attention_groups(pooled, qkv_weight, out_weight)
     return (pooled, update)
 

time: 208 us -> 143 us (0.69)
  waiting for transfers between devices: 109 us -> 0 us
  Pallas kernels: 77.7 us -> 135 us
  between operations: 14.1 us -> 0.66 us
  local copies, waits for them, and re-layouts: 7.24 us -> 4.28 us
  other arithmetic: 0 us -> 2.69 us
    all_gather x2 -> x0, waiting for transfers between devices: 107 us -> none  [the longest x1 91.3 us: on_device(): lax.all_gather(qkv_weight, 'seq', axis=0, tiled=True)]
    pallas_call x1, Pallas kernels: 22.5 us -> 80.4 us  [conv_pool(): pl.pallas_call(functools.partial(conv_kernel, count, share), out_shape=ou...]
    concatenate x0 -> x1, other arithmetic: none -> 2.69 us  [on_device(): jnp.concatenate([qkv_weight, jnp.concatenate([out_weight[:part], out_weig...]
    reshape x1, local copies, waits for them, and re-layouts: 3.59 us -> 1.46 us  [conv_pool(): pairs = sequence.reshape(half, 2 * d)]
  transfers between devices with their start and end apart: 2 -> 0, of which waited for: 2 -> 0; matrix products, arithmetic and copies ran while one was open for 2% -> 0% of each run, Pallas kernels for 11% -> 0%
where the time goes in v2:
time: 143 us
  Pallas kernels  135 us (94%)
  local copies, waits for them, and re-layouts  4.28 us (3%)
  other arithmetic  2.69 us (2%)
    pallas_call x1, Pallas kernels, conv_pool(): pl.pallas_call(functools.partial(conv_kernel, count, share), out_shape=ou...  80.4 us
    pallas_call x1, Pallas kernels, attention(): pl.pallas_call(attend_kernel, out_shape=jax.ShapeDtypeStruct((count, d),...  55 us

profile of v2, /device:TPU:0, one launch (start us, length us, event | category | flops | bytes accessed | tf_op | source)
XLA Modules:
  0.0 143.0 jit_solution(591345271331914164)
XLA Ops:
  0.6 1.0 fusion
  1.7 0.0 copy-start
  1.7 2.7 %maximum_maximum_fusion.refs_2_ = bf16[256,3072]{1,0:T(8,128)(2,1)} fusion(bf16[64,1536]{1,0:T(8,128)(2,1)S(1)} %get-tuple-element.7, bf16[64,1536]{1,0:T(8,128)(2,1)S(1)} %get-tuple-element.6, bf16[192,3072]{1,0:T(8,128)(2,1)} %param.6), kind=kLoop, calls=%fused_computation | loop fusion | flops 4718592 | bytes 3145728 | tf_op jit(solution)/shard_map/concatenate | solution.py:557
  4.4 0.0 copy-done
  4.4 1.5 %reshape.10.refs_0_ = bf16[256,3072]{1,0:T(8,128)(2,1)} reshape(bf16[512,1536]{1,0:T(8,128)(2,1)S(1)} %copy-done) | data formatting | bytes 3145728 | tf_op jit(solution)/shard_map/reshape | solution.py:278
  5.8 80.4 %conv_pool.1 = (bf16[256,1536]{1,0:T(8,128)(2,1)S(1)}, bf16[8,256,3072]{2,1,0:T(8,128)(2,1)}) custom-call(bf16[256,3072]{1,0:T(8,128)(2,1)} %reshape.10.refs_0_, bf16[7680,1536]{1,0:T(8,128)(2,1)} %bitcast.1, bf16[256,3072]{1,0:T(8,128)(2,1)} %maximum_maximum_fusion.refs_2_), custom_call_target="tpu_custom_call" | custom-call | flops 12079595520 | bytes 23592960 | tf_op jit(solution)/shard_map/conv_pool/pallas_call | solution.py:292
  86.3 55.0 %attend.1 = bf16[256,1536]{1,0:T(8,128)(2,1)S(1)} custom-call(bf16[256,1536]{1,0:T(8,128)(2,1)S(1)} %get-tuple-element.10.pooled_ref, bf16[8,256,3072]{2,1,0:T(8,128)(2,1)} %get-tuple-element.5.w_ref), custom_call_target="tpu_custom_call" | custom-call | flops 5368709120 | bytes 12582912 | tf_op jit(solution)/shard_map/attend/pallas_call | solution.py:456
  141.3 0.9 copy.8
  142.2 0.9 copy.9
Async XLA Ops:
  1.7 2.7 %copy-start = (bf16[512,1536]{1,0:T(8,128)(2,1)S(1)}, bf16[512,1536]{1,0:T(8,128)(2,1)}, u32[]{:S(2)}) copy-start(bf16[512,1536]{1,0:T(8,128)(2,1)} %param.4) | copy-start | bytes 4718596

commit v3 on v2

--- a/solution.py
+++ b/solution.py
@@ -16,6 +16,7 @@
 DP = 4
 PAIRS = 4
 REMOTE = 6
+WINDOW = 2
 
 
 class Gather:
@@ -101,9 +102,15 @@
             self.out1(i).start()
             return 0
 
-        lax.fori_loop(0, REMOTE, one, 0)
+        lax.fori_loop(0, WINDOW, one, 0)
 
     def relay(self, i):
+        self.out1(i).wait_send()
+
+        @pl.when(i + WINDOW < REMOTE)
+        def _():
+            self.out1(i + WINDOW).start()
+
         self.in1(i).wait_recv()
         for j in range(1, DP):
             self.out2(i, j).start()
@@ -119,7 +126,6 @@
         lax.fori_loop(0, REMOTE, second, 0)
 
         def last(i, _):
-            self.out1(i).wait_send()
             for j in range(1, DP):
                 self.out2(i, j).wait_send()
             for group in range(DP):
@@ -256,14 +262,14 @@
     lax.fori_loop(0, chunks, place, 0)
 
     def conv_step(c, _):
+        if share:
+            gather.relay(c)
         w_copy(c).wait()
         k = pl.multiple_of(c * step, step)
         mixed = jnp.dot(taps[...], wbuf[c], preferred_element_type=jnp.float32)
         even = mixed[:half] + seq_ref[:, pl.ds(k, step)].astype(jnp.float32)
         odd = mixed[half:] + seq_ref[:, pl.ds(k + d, step)].astype(jnp.float32)
         pooled_ref[:, pl.ds(k, step)] = jnp.maximum(even, odd).astype(jnp.bfloat16)
-        if share:
-            gather.relay(c)
         return 0
 
     lax.fori_loop(0, chunks, conv_step, 0)

time: 143 us -> 143 us (level)
    pallas_call x1, Pallas kernels: 55 us -> 59.3 us  [attention(): pl.pallas_call(attend_kernel, out_shape=jax.ShapeDtypeStruct((count, d),...]
    pallas_call x1, Pallas kernels: 80.4 us -> 76.3 us  [conv_pool(): pl.pallas_call(functools.partial(conv_kernel, count, share), out_shape=ou...]
where the time goes in v3:
time: 143 us
  Pallas kernels  136 us (95%)
  local copies, waits for them, and re-layouts  4.28 us (3%)
  other arithmetic  2.69 us (2%)
    pallas_call x1, Pallas kernels, conv_pool(): pl.pallas_call(functools.partial(conv_kernel, count, share), out_shape=ou...  76.3 us
    pallas_call x1, Pallas kernels, attention(): pl.pallas_call(attend_kernel, out_shape=jax.ShapeDtypeStruct((count, d),...  59.3 us

profile of v3, /device:TPU:0, one launch (start us, length us, event | category | flops | bytes accessed | tf_op | source)
XLA Modules:
  0.0 143.2 jit_solution(16565130616481818142)
XLA Ops:
  0.6 1.0 fusion
  1.7 0.0 copy-start
  1.7 2.7 %maximum_maximum_fusion.refs_2_ = bf16[256,3072]{1,0:T(8,128)(2,1)} fusion(bf16[64,1536]{1,0:T(8,128)(2,1)S(1)} %get-tuple-element.7, bf16[64,1536]{1,0:T(8,128)(2,1)S(1)} %get-tuple-element.6, bf16[192,3072]{1,0:T(8,128)(2,1)} %param.6), kind=kLoop, calls=%fused_computation | loop fusion | flops 4718592 | bytes 3145728 | tf_op jit(solution)/shard_map/concatenate | solution.py:563
  4.4 0.0 copy-done
  4.4 1.5 %reshape.10.refs_0_ = bf16[256,3072]{1,0:T(8,128)(2,1)} reshape(bf16[512,1536]{1,0:T(8,128)(2,1)S(1)} %copy-done) | data formatting | bytes 3145728 | tf_op jit(solution)/shard_map/reshape | solution.py:284
  5.8 76.3 %conv_pool.1 = (bf16[256,1536]{1,0:T(8,128)(2,1)S(1)}, bf16[8,256,3072]{2,1,0:T(8,128)(2,1)}) custom-call(bf16[256,3072]{1,0:T(8,128)(2,1)} %reshape.10.refs_0_, bf16[7680,1536]{1,0:T(8,128)(2,1)} %bitcast.1, bf16[256,3072]{1,0:T(8,128)(2,1)} %maximum_maximum_fusion.refs_2_), custom_call_target="tpu_custom_call" | custom-call | flops 12079595520 | bytes 23592960 | tf_op jit(solution)/shard_map/conv_pool/pallas_call | solution.py:298
  82.1 59.3 %attend.1 = bf16[256,1536]{1,0:T(8,128)(2,1)S(1)} custom-call(bf16[256,1536]{1,0:T(8,128)(2,1)S(1)} %get-tuple-element.10.pooled_ref, bf16[8,256,3072]{2,1,0:T(8,128)(2,1)} %get-tuple-element.5.w_ref), custom_call_target="tpu_custom_call" | custom-call | flops 5368709120 | bytes 12582912 | tf_op jit(solution)/shard_map/attend/pallas_call | solution.py:462
  141.4 0.9 copy.8
  142.3 0.9 copy.9
Async XLA Ops:
  1.7 2.7 %copy-start = (bf16[512,1536]{1,0:T(8,128)(2,1)S(1)}, bf16[512,1536]{1,0:T(8,128)(2,1)}, u32[]{:S(2)}) copy-start(bf16[512,1536]{1,0:T(8,128)(2,1)} %param.4) | copy-start | bytes 4718596

commit v4 on v3

--- a/solution.py
+++ b/solution.py
@@ -319,26 +319,20 @@
     )(*operands)
 
 
-def attend_kernel(pooled_ref, w_ref, update_ref, normed, wbuf, owbuf, send, recv, att_send, att_recv,
+def attend_kernel(pooled_ref, w_ref, out_w_ref, update_ref, normed, wbuf, owbuf, send, recv, att_send, att_recv,
                   send_sem, recv_sem, asend_sem, arecv_sem, w_sem):
     me = lax.axis_index("seq")
     count, d = pooled_ref.shape
     inner = HEADS * HEAD_DIM
-    depth = d // HEADS
 
     def w_copy(t):
-        return pltpu.make_async_copy(
-            w_ref.at[:, pl.ds(0, depth), pl.ds(t * inner, inner)], wbuf.at[t], w_sem.at[t])
-
-    def ow_copy(part):
-        return pltpu.make_async_copy(
-            w_ref.at[:, pl.ds(depth, HEAD_DIM // 2), pl.ds(part * d, d)], owbuf.at[:, part], w_sem.at[3 + part])
-
+        return pltpu.make_async_copy(w_ref.at[:, :, pl.ds(t * inner, inner)], wbuf.at[t], w_sem.at[t])
+
+    ow_copy = pltpu.make_async_copy(out_w_ref, owbuf, w_sem.at[3])
     order = (1, 2, 0)
     for t in order:
         w_copy(t).start()
-    for part in range(2):
-        ow_copy(part).start()
+    ow_copy.start()
 
     barrier = pltpu.get_barrier_semaphore()
 
@@ -446,16 +440,15 @@
         return 0
 
     lax.fori_loop(1, HEADS, finish, 0)
-    for part in range(2):
-        ow_copy(part).wait()
+    ow_copy.wait()
     joined = jnp.concatenate([att_recv[h] for h in range(HEADS)], axis=1)
     for p in range(d // 512):
         update_ref[:, p * 512 : (p + 1) * 512] = jnp.dot(
-            joined, owbuf[:, :, :, p * 512 : (p + 1) * 512].reshape(inner, 512), preferred_element_type=jnp.float32
+            joined, owbuf[:, p * 512 : (p + 1) * 512], preferred_element_type=jnp.float32
         ).astype(jnp.bfloat16)
 
 
-def attention(pooled, weights):
+def attention(pooled, weights, out_weight):
     count, d = pooled.shape
     inner = HEADS * HEAD_DIM
     heads = (HEADS, count, HEAD_DIM)
@@ -465,12 +458,13 @@
         in_specs=[
             pl.BlockSpec(memory_space=pltpu.VMEM),
             pl.BlockSpec(memory_space=pl.ANY),
+            pl.BlockSpec(memory_space=pl.ANY),
         ],
         out_specs=pl.BlockSpec(memory_space=pltpu.VMEM),
         scratch_shapes=[
             pltpu.VMEM((count, d), jnp.bfloat16),
             pltpu.VMEM((3, HEADS, d // HEADS, inner), jnp.bfloat16),
-            pltpu.VMEM((HEADS, 2, HEAD_DIM // 2, d), jnp.bfloat16),
+            pltpu.VMEM((inner, d), jnp.bfloat16),
             pltpu.VMEM((3,) + heads, jnp.bfloat16),
             pltpu.VMEM((3,) + heads, jnp.bfloat16),
             pltpu.VMEM(heads, jnp.bfloat16),
@@ -479,7 +473,7 @@
             pltpu.SemaphoreType.DMA((3, HEADS)),
             pltpu.SemaphoreType.DMA((HEADS,)),
             pltpu.SemaphoreType.DMA((HEADS,)),
-            pltpu.SemaphoreType.DMA((5,)),
+            pltpu.SemaphoreType.DMA((4,)),
         ],
         compiler_params=pltpu.CompilerParams(
             collective_id=1, has_side_effects=True, vmem_limit_bytes=44 * MB),
@@ -487,7 +481,7 @@
             flops=2 * count * d * 4 * inner + 4 * count * HEADS * count * inner,
             bytes_accessed=8 * d * inner, transcendentals=count * count * HEADS * HEADS),
         name="attend",
-    )(pooled, weights)
+    )(pooled, weights, out_weight)
 
 
 def normalize(values):
@@ -559,11 +553,9 @@
 def on_device(sequence, conv_weight, qkv_weight, out_weight):
     count = lax.axis_size("seq")
     if count == HEADS and lax.axis_size("dp") == DP:
-        part = out_weight.shape[0] // 2
-        shard = jnp.concatenate(
-            [qkv_weight, jnp.concatenate([out_weight[:part], out_weight[part:]], axis=1)], axis=0)
-        pooled, weights = conv_pool(sequence, conv_weight, count, shard)
-        update = attention(pooled, weights)
+        outer = lax.all_gather(out_weight, "seq", axis=0, tiled=True)
+        pooled, weights = conv_pool(sequence, conv_weight, count, qkv_weight)
+        update = attention(pooled, weights, outer)
     else:
         pooled = conv_pool(sequence, conv_weight, count)
         update = attention_groups(pooled, qkv_weight, out_weight)

time: 143 us -> 161 us (1.13)
  between operations: 0.66 us -> 14.1 us
  local copies, waits for them, and re-layouts: 4.28 us -> 7.23 us
  other arithmetic: 2.69 us -> 0 us
  Pallas kernels: 136 us -> 138 us
    pallas_call x1, Pallas kernels: 76.3 us -> 82.9 us  [conv_pool(): pl.pallas_call(functools.partial(conv_kernel, count, share), out_shape=ou...]
    pallas_call x1, Pallas kernels: 59.3 us -> 55.2 us  [attention(): pl.pallas_call(attend_kernel, out_shape=jax.ShapeDtypeStruct((count, d),...]
    concatenate x1 -> x0, other arithmetic: 2.69 us -> none  [on_device(): jnp.concatenate([qkv_weight, jnp.concatenate([out_weight[:part], out_weig...]
    reshape x1, local copies, waits for them, and re-layouts: 1.46 us -> 3.58 us  [conv_pool(): pairs = sequence.reshape(half, 2 * d)]
    unnamed x4 -> x6, local copies, waits for them, and re-layouts: 1.77 us -> 3.65 us
  transfers between devices with their start and end apart: 0 -> 1, of which waited for: 0 -> 0; matrix products, arithmetic and copies ran while one was open for 0% -> 2% of each run, Pallas kernels for 0% -> 52%
where the time goes in v4:
time: 161 us; the launch traced here: 160 us
  Pallas kernels  138 us (86%)
  between operations  14.1 us (9%)
  local copies, waits for them, and re-layouts  7.23 us (4%)
    pallas_call x1, Pallas kernels, conv_pool(): pl.pallas_call(functools.partial(conv_kernel, count, share), out_shape=ou...  82.9 us
    pallas_call x1, Pallas kernels, attention(): pl.pallas_call(attend_kernel, out_shape=jax.ShapeDtypeStruct((count, d),...  55.2 us
    unnamed x6, local copies, waits for them, and re-layouts  3.65 us
    reshape x1, local copies, waits for them, and re-layouts, conv_pool(): pairs = sequence.reshape(half, 2 * d)  3.58 us
  transfers between devices with their start and end apart: 1, of which 0 were waited for; matrix products, arithmetic and copies ran while one was open for 2% of the time, Pallas kernels for 52%

profile of v4, /device:TPU:0, one launch (start us, length us, event | category | flops | bytes accessed | tf_op | source)
XLA Modules:
  0.0 160.1 jit_solution(12619926295279748615)
XLA Ops:
  7.2 0.0 copy-start.1
  7.2 0.0 all-gather.2.cloned.1.call-start
  7.2 0.7 all-gather.2.cloned.1.call-update
  7.9 3.6 %reshape.10.refs_0_ = bf16[256,3072]{1,0:T(8,128)(2,1)} reshape(bf16[512,1536]{1,0:T(8,128)(2,1)} %param.4) | data formatting | bytes 3145728 | tf_op jit(solution)/shard_map/reshape | solution.py:284
  11.5 0.0 copy-done.1
  11.5 82.9 %conv_pool.1 = (bf16[256,1536]{1,0:T(8,128)(2,1)S(1)}, bf16[8,192,3072]{2,1,0:T(8,128)(2,1)}) custom-call(bf16[256,3072]{1,0:T(8,128)(2,1)} %reshape.10.refs_0_, bf16[7680,1536]{1,0:T(8,128)(2,1)} %bitcast.1, bf16[192,3072]{1,0:T(8,128)(2,1)S(1)} %copy-done.1), custom_call_target="tpu_custom_call" | custom-call | flops 12079595520 | bytes 23592960 | tf_op jit(solution)/shard_map/conv_pool/pallas_call | solution.py:298
  94.4 0.0 all-gather.2.cloned.1.call-done.out_w_ref
  94.4 0.0 copy-start
  94.4 1.9 %copy-done = bf16[1024,1536]{1,0:T(8,128)(2,1)S(1)} copy-done((bf16[1024,1536]{1,0:T(8,128)(2,1)S(1)}, bf16[1024,1536]{1,0:T(8,128)(2,1)}, u32[]{:S(2)}) %copy-start) | copy-done | bytes 3145752
  96.3 55.2 %attend.1 = bf16[256,1536]{1,0:T(8,128)(2,1)S(1)} custom-call(bf16[256,1536]{1,0:T(8,128)(2,1)S(1)} %get-tuple-element.8.pooled_ref, bf16[8,192,3072]{2,1,0:T(8,128)(2,1)} %get-tuple-element.5.w_ref, bf16[1024,1536]{1,0:T(8,128)(2,1)S(1)} %copy-done), custom_call_target="tpu_custom_call" | custom-call | flops 5368709120 | bytes 12582912 | tf_op jit(solution)/shard_map/attend/pallas_call | solution.py:455
  151.5 0.9 copy.8
  152.4 0.9 copy.9
Async XLA Ops:
  7.2 4.3 %copy-start.1 = (bf16[192,3072]{1,0:T(8,128)(2,1)S(1)}, bf16[192,3072]{1,0:T(8,128)(2,1)}, u32[]{:S(2)}) copy-start(bf16[192,3072]{1,0:T(8,128)(2,1)} %refs_2_.1) | copy-start | bytes 3538948
  7.2 87.3 %all-gather.2.cloned.1.call-start = ((), (), s32[]{:S(2)}) async-start(), calls=%async_computation | async-start | bytes 3538944 | tf_op jit(solution)/shard_map/all_gather | solution.py:556
  94.4 1.9 %copy-start = (bf16[1024,1536]{1,0:T(8,128)(2,1)S(1)}, bf16[1024,1536]{1,0:T(8,128)(2,1)}, u32[]{:S(2)}) copy-start(bf16[1024,1536]{1,0:T(8,128)(2,1)} %all-gather.2.cloned.1.call-done.out_w_ref) | copy-start | bytes 9437188
Sparse Core Ops, SparseCore 0:
  9.6 63.3 all-gather.1

commit v5 on v3

--- a/solution.py
+++ b/solution.py
@@ -17,6 +17,7 @@
 PAIRS = 4
 REMOTE = 6
 WINDOW = 2
+LAG = 2
 
 
 class Gather:
@@ -27,11 +28,11 @@
         self.dp = lax.axis_index("dp")
         self.pair, self.core = self.me // 2, self.me % 2
         self.mate = self.pair * 2 + 1 - self.core
-        self.width = whole.shape[2] // (2 * DP)
+        self.width = whole.shape[1] // (2 * DP)
 
     def part(self, source, group, core):
-        first = pl.multiple_of((2 * group + core) * self.width, 128)
-        return self.whole.at[source, :, pl.ds(first, self.width)]
+        first = pl.multiple_of((2 * group + core) * self.width, self.width)
+        return self.whole.at[source, pl.ds(first, self.width)]
 
     def own(self):
         return pltpu.make_async_copy(self.shard, self.whole.at[self.me], self.own_sem.at[0])
@@ -54,9 +55,9 @@
 
     def out1(self, i):
         peer = self.target(i)
-        first = pl.multiple_of((2 * self.dp + peer % 2) * self.width, 128)
-        return pltpu.make_async_remote_copy(
-            src_ref=self.shard.at[:, pl.ds(first, self.width)], dst_ref=self.part(self.me, self.dp, peer % 2),
+        first = pl.multiple_of((2 * self.dp + peer % 2) * self.width, self.width)
+        return pltpu.make_async_remote_copy(
+            src_ref=self.shard.at[pl.ds(first, self.width)], dst_ref=self.part(self.me, self.dp, peer % 2),
             send_sem=self.s1.at[peer], recv_sem=self.r1.at[self.me], device_id={"seq": peer}, device_id_type=MESH)
 
     def in1(self, i):
@@ -116,14 +117,17 @@
             self.out2(i, j).start()
         self.out3(i, self.dp).start()
 
+    def second(self, i):
+        for j in range(1, DP):
+            self.in2(i, j).wait_recv()
+            self.out3(i, (self.dp + j) % DP).start()
+
     def finish(self):
-        def second(i, _):
-            for j in range(1, DP):
-                self.in2(i, j).wait_recv()
-                self.out3(i, (self.dp + j) % DP).start()
+        def rest(i, _):
+            self.second(i)
             return 0
 
-        lax.fori_loop(0, REMOTE, second, 0)
+        lax.fori_loop(REMOTE - LAG, REMOTE, rest, 0)
 
         def last(i, _):
             for j in range(1, DP):
@@ -264,6 +268,11 @@
     def conv_step(c, _):
         if share:
             gather.relay(c)
+
+            @pl.when(c >= LAG)
+            def _():
+                gather.second(c - LAG)
+
         w_copy(c).wait()
         k = pl.multiple_of(c * step, step)
         mixed = jnp.dot(taps[...], wbuf[c], preferred_element_type=jnp.float32)

time: 143 us -> 143 us (level)
  no operation moved by 1% of the time
where the time goes in v5:
time: 143 us
  Pallas kernels  136 us (95%)
  local copies, waits for them, and re-layouts  4.28 us (3%)
  other arithmetic  2.69 us (2%)
    pallas_call x1, Pallas kernels, conv_pool(): pl.pallas_call(functools.partial(conv_kernel, count, share), out_shape=ou...  76.3 us
    pallas_call x1, Pallas kernels, attention(): pl.pallas_call(attend_kernel, out_shape=jax.ShapeDtypeStruct((count, d),...  59.3 us

profile of v5, /device:TPU:0, one launch (start us, length us, event | category | flops | bytes accessed | tf_op | source)
XLA Modules:
  0.0 143.2 jit_solution(17725866863895107379)
XLA Ops:
  0.6 1.0 fusion
  1.7 0.0 copy-start
  1.7 2.7 %maximum_maximum_fusion.refs_2_ = bf16[256,3072]{1,0:T(8,128)(2,1)} fusion(bf16[64,1536]{1,0:T(8,128)(2,1)S(1)} %get-tuple-element.7, bf16[64,1536]{1,0:T(8,128)(2,1)S(1)} %get-tuple-element.6, bf16[192,3072]{1,0:T(8,128)(2,1)} %param.6), kind=kLoop, calls=%fused_computation | loop fusion | flops 4718592 | bytes 3145728 | tf_op jit(solution)/shard_map/concatenate | solution.py:572
  4.4 0.0 copy-done
  4.4 1.5 %reshape.10.refs_0_ = bf16[256,3072]{1,0:T(8,128)(2,1)} reshape(bf16[512,1536]{1,0:T(8,128)(2,1)S(1)} %copy-done) | data formatting | bytes 3145728 | tf_op jit(solution)/shard_map/reshape | solution.py:293
  5.8 76.3 %conv_pool.1 = (bf16[256,1536]{1,0:T(8,128)(2,1)S(1)}, bf16[8,256,3072]{2,1,0:T(8,128)(2,1)}) custom-call(bf16[256,3072]{1,0:T(8,128)(2,1)} %reshape.10.refs_0_, bf16[7680,1536]{1,0:T(8,128)(2,1)} %bitcast.1, bf16[256,3072]{1,0:T(8,128)(2,1)} %maximum_maximum_fusion.refs_2_), custom_call_target="tpu_custom_call" | custom-call | flops 12079595520 | bytes 23592960 | tf_op jit(solution)/shard_map/conv_pool/pallas_call | solution.py:307
  82.1 59.3 %attend.1 = bf16[256,1536]{1,0:T(8,128)(2,1)S(1)} custom-call(bf16[256,1536]{1,0:T(8,128)(2,1)S(1)} %get-tuple-element.10.pooled_ref, bf16[8,256,3072]{2,1,0:T(8,128)(2,1)} %get-tuple-element.5.w_ref), custom_call_target="tpu_custom_call" | custom-call | flops 5368709120 | bytes 12582912 | tf_op jit(solution)/shard_map/attend/pallas_call | solution.py:471
  141.4 0.9 copy.8
  142.3 0.9 copy.9
Async XLA Ops:
  1.7 2.7 %copy-start = (bf16[512,1536]{1,0:T(8,128)(2,1)S(1)}, bf16[512,1536]{1,0:T(8,128)(2,1)}, u32[]{:S(2)}) copy-start(bf16[512,1536]{1,0:T(8,128)(2,1)} %param.4) | copy-start | bytes 4718596

commit v6 on v5

--- a/solution.py
+++ b/solution.py
@@ -21,13 +21,15 @@
 
 
 class Gather:
-    def __init__(self, shard, whole, sems):
-        self.shard, self.whole = shard, whole
-        self.s1, self.r1, self.s2, self.r2, self.s3, self.r3, self.own_sem = sems
+    def __init__(self, first, second, whole, sems):
+        self.first, self.last, self.whole = first, second, whole
+        self.s1, self.r1, self.s2, self.r2, self.s3, self.r3, self.s4, self.own_sem = sems
         self.me = lax.axis_index("seq")
         self.dp = lax.axis_index("dp")
         self.pair, self.core = self.me // 2, self.me % 2
         self.mate = self.pair * 2 + 1 - self.core
+        self.shard = whole.at[self.me]
+        self.mates = (self.dp, self.dp + 1 - 2 * (self.dp % 2), (self.dp + 2) % DP, DP - 1 - self.dp)
         self.width = whole.shape[1] // (2 * DP)
 
     def part(self, source, group, core):
@@ -35,7 +37,14 @@
         return self.whole.at[source, pl.ds(first, self.width)]
 
     def own(self):
-        return pltpu.make_async_copy(self.shard, self.whole.at[self.me], self.own_sem.at[0])
+        depth, wide = self.first.shape
+        part = self.last.shape[0] // 2
+        copies = [pltpu.make_async_copy(self.first, self.shard.at[pl.ds(0, depth)], self.own_sem.at[0])]
+        for k in range(2):
+            copies.append(pltpu.make_async_copy(
+                self.last.at[pl.ds(k * part, part)],
+                self.shard.at[pl.ds(depth, part), pl.ds(k * wide // 2, wide // 2)], self.own_sem.at[k + 1]))
+        return copies
 
     def to_mate(self):
         return pltpu.make_async_remote_copy(
@@ -60,6 +69,13 @@
             src_ref=self.shard.at[pl.ds(first, self.width)], dst_ref=self.part(self.me, self.dp, peer % 2),
             send_sem=self.s1.at[peer], recv_sem=self.r1.at[self.me], device_id={"seq": peer}, device_id_type=MESH)
 
+    def out4(self, i):
+        peer, group = self.target(i), self.mates[3]
+        block = self.part(self.me, group, peer % 2)
+        return pltpu.make_async_remote_copy(
+            src_ref=block, dst_ref=block, send_sem=self.s4.at[peer], recv_sem=self.r2.at[self.me, group],
+            device_id={"seq": peer}, device_id_type=MESH)
+
     def in1(self, i):
         source = self.source(i)
         block = self.part(source, self.dp, self.core)
@@ -68,14 +84,14 @@
             device_id={"seq": source}, device_id_type=MESH)
 
     def out2(self, i, j):
-        source, peer = self.source(i), (self.dp + j) % DP
+        source, peer = self.source(i), self.mates[j]
         block = self.part(source, self.dp, self.core)
         return pltpu.make_async_remote_copy(
             src_ref=block, dst_ref=block, send_sem=self.s2.at[source, peer], recv_sem=self.r2.at[source, self.dp],
             device_id={"dp": peer}, device_id_type=MESH)
 
     def in2(self, i, j):
-        source, peer = self.source(i), (self.dp + j) % DP
+        source, peer = self.source(i), self.mates[j]
         block = self.part(source, peer, self.core)
         return pltpu.make_async_remote_copy(
             src_ref=block, dst_ref=block, send_sem=self.s2.at[source, peer], recv_sem=self.r2.at[source, peer],
@@ -96,13 +112,15 @@
             device_id={"seq": self.mate}, device_id_type=MESH)
 
     def start(self):
-        self.own().start()
+        for copy in self.own():
+            copy.wait()
         self.to_mate().start()
 
         def one(i, _):
             self.out1(i).start()
             return 0
 
+
         lax.fori_loop(0, WINDOW, one, 0)
 
     def relay(self, i):
@@ -113,14 +131,23 @@
             self.out1(i + WINDOW).start()
 
         self.in1(i).wait_recv()
-        for j in range(1, DP):
+        for j in range(1, DP - 1):
             self.out2(i, j).start()
+
+        @pl.when(self.core == 0)
+        def _():
+            self.out4(i).start()
+
+        @pl.when(i % 2 == 1)
+        def _():
+            self.out2(i, DP - 1).start()
+
         self.out3(i, self.dp).start()
 
     def second(self, i):
         for j in range(1, DP):
             self.in2(i, j).wait_recv()
-            self.out3(i, (self.dp + j) % DP).start()
+            self.out3(i, self.mates[j]).start()
 
     def finish(self):
         def rest(i, _):
@@ -130,26 +157,37 @@
         lax.fori_loop(REMOTE - LAG, REMOTE, rest, 0)
 
         def last(i, _):
-            for j in range(1, DP):
+            for j in range(1, DP - 1):
                 self.out2(i, j).wait_send()
+
+            @pl.when(self.core == 0)
+            def _():
+                self.out4(i).wait_send()
+
+            @pl.when(i % 2 == 1)
+            def _():
+                self.out2(i, DP - 1).wait_send()
+
             for group in range(DP):
                 self.out3(i, group).wait_send()
                 self.in3(i, group).wait_recv()
             return 0
 
         lax.fori_loop(0, REMOTE, last, 0)
-        self.own().wait()
         self.to_mate().wait_send()
         self.from_mate().wait_recv()
 
 
 def conv_kernel(count, share, *refs):
     if share:
-        seq_ref, w_ref, shard, pooled_ref, whole, *refs = refs
+        seq_ref, w_ref, first, second, pooled_ref, whole, *refs = refs
     else:
         seq_ref, w_ref, pooled_ref, *refs = refs
     low, high, wbuf, ebuf, obuf, taps, send_sem, recv_sem, w_sem, *sems = refs
-    gather = Gather(shard, whole, sems) if share else None
+    gather = Gather(first, second, whole, sems) if share else None
+    if share:
+        for copy in gather.own():
+            copy.start()
     me = lax.axis_index("seq")
     half, wide = seq_ref.shape
     d = wide // 2
@@ -298,12 +336,12 @@
     in_specs = [pl.BlockSpec(memory_space=pltpu.VMEM), pl.BlockSpec(memory_space=pl.ANY)]
     operands, sems = [pairs, weight], []
     if share:
-        out_shape = (out_shape, jax.ShapeDtypeStruct((count,) + shard.shape, jnp.bfloat16))
+        out_shape = (out_shape, jax.ShapeDtypeStruct((count, shard[0].shape[0] + shard[1].shape[0] // 2, 2 * d), jnp.bfloat16))
         out_specs = (out_specs, pl.BlockSpec(memory_space=pl.ANY))
-        in_specs.append(pl.BlockSpec(memory_space=pl.ANY))
-        operands.append(shard)
+        in_specs += [pl.BlockSpec(memory_space=pl.ANY)] * 2
+        operands += shard
         sems = [pltpu.SemaphoreType.DMA((count,))] * 2 + [pltpu.SemaphoreType.DMA((count, DP))] * 4
-        sems.append(pltpu.SemaphoreType.DMA((1,)))
+        sems += [pltpu.SemaphoreType.DMA((count,)), pltpu.SemaphoreType.DMA((3,))]
     return pl.pallas_call(
         functools.partial(conv_kernel, count, share),
         out_shape=out_shape,
@@ -568,10 +606,7 @@
 def on_device(sequence, conv_weight, qkv_weight, out_weight):
     count = lax.axis_size("seq")
     if count == HEADS and lax.axis_size("dp") == DP:
-        part = out_weight.shape[0] // 2
-        shard = jnp.concatenate(
-            [qkv_weight, jnp.concatenate([out_weight[:part], out_weight[part:]], axis=1)], axis=0)
-        pooled, weights = conv_pool(sequence, conv_weight, count, shard)
+        pooled, weights = conv_pool(sequence, conv_weight, count, [qkv_weight, out_weight])
         update = attention(pooled, weights)
     else:
         pooled = conv_pool(sequence, conv_weight, count)

time: 143 us -> 173 us (1.21); the launches traced: 143 us -> 171 us
  Pallas kernels: 136 us -> 165 us
  other arithmetic: 2.69 us -> 0 us
    pallas_call x1, Pallas kernels: 76.3 us -> 109 us  [conv_pool(): pl.pallas_call(functools.partial(conv_kernel, count, share), out_shape=ou...]
    pallas_call x1, Pallas kernels: 59.3 us -> 55.5 us  [attention(): pl.pallas_call(attend_kernel, out_shape=jax.ShapeDtypeStruct((count, d),...]
    concatenate x1 -> x0, other arithmetic: 2.69 us -> none  [on_device(): jnp.concatenate([qkv_weight, jnp.concatenate([out_weight[:part], out_weig...]
    reshape x1, local copies, waits for them, and re-layouts: 1.46 us -> 3.62 us  [conv_pool(): pairs = sequence.reshape(half, 2 * d)]
where the time goes in v6:
time: 173 us; the launch traced here: 171 us
  Pallas kernels  165 us (95%)
  local copies, waits for them, and re-layouts  5.38 us (3%)
    pallas_call x1, Pallas kernels, conv_pool(): pl.pallas_call(functools.partial(conv_kernel, count, share), out_shape=ou...  109 us
    pallas_call x1, Pallas kernels, attention(): pl.pallas_call(attend_kernel, out_shape=jax.ShapeDtypeStruct((count, d),...  55.5 us
    reshape x1, local copies, waits for them, and re-layouts, conv_pool(): pairs = sequence.reshape(half, 2 * d)  3.62 us

profile of v6, /device:TPU:0, one launch (start us, length us, event | category | flops | bytes accessed | tf_op | source)
XLA Modules:
  0.0 170.8 jit_solution(2838145565627440015)
XLA Ops:
  0.6 0.0 copy-start
  0.6 3.6 %reshape.10.refs_0_ = bf16[256,3072]{1,0:T(8,128)(2,1)} reshape(bf16[512,1536]{1,0:T(8,128)(2,1)} %param.4) | data formatting | bytes 3145728 | tf_op jit(solution)/shard_map/reshape | solution.py:331
  4.3 0.0 copy-done
  4.3 109.3 %conv_pool.1 = (bf16[256,1536]{1,0:T(8,128)(2,1)S(1)}, bf16[8,256,3072]{2,1,0:T(8,128)(2,1)}) custom-call(bf16[256,3072]{1,0:T(8,128)(2,1)} %reshape.10.refs_0_, bf16[7680,1536]{1,0:T(8,128)(2,1)} %bitcast.1, bf16[192,3072]{1,0:T(8,128)(2,1)} %refs_2_.1, bf16[128,1536]{1,0:T(8,128)(2,1)S(1)} %copy-done), custom_call_target="tpu_custom_call" | custom-call | flops 12079595520 | bytes 23592960 | tf_op jit(solution)/shard_map/conv_pool/pallas_call | solution.py:345
  113.6 55.5 %attend.1 = bf16[256,1536]{1,0:T(8,128)(2,1)S(1)} custom-call(bf16[256,1536]{1,0:T(8,128)(2,1)S(1)} %get-tuple-element.8.pooled_ref, bf16[8,256,3072]{2,1,0:T(8,128)(2,1)} %get-tuple-element.5.w_ref), custom_call_target="tpu_custom_call" | custom-call | flops 5368709120 | bytes 12582912 | tf_op jit(solution)/shard_map/attend/pallas_call | solution.py:509
  169.1 0.9 copy.8
  169.9 0.9 copy.9
Async XLA Ops:
  0.6 3.6 %copy-start = (bf16[128,1536]{1,0:T(8,128)(2,1)S(1)}, bf16[128,1536]{1,0:T(8,128)(2,1)}, u32[]{:S(2)}) copy-start(bf16[128,1536]{1,0:T(8,128)(2,1)} %refs_3_.1) | copy-start | bytes 1179652
